TPU v7x, 512 devices: a whole 4x8x8 slice. The times are simulated.
512 devices in a mesh: node: 64 (over z, x, core), local: 8 (over y).
Axes of the slice: x: 4, y: 8, z: 8, core: 2. Of those that a mesh axis runs over, the one named last changes fastest.
Arguments:
- input_activation_matrix: bfloat16 [65536, 1024], P(('node', 'local')), may hold values from -6 to 6
- output_adjoint: bfloat16 [65536, 1024], P(('node', 'local')), may hold values from -6 to 6
- dispatch_mixing_factors: bfloat16 [65536, 8], P(('node', 'local')), may hold values from 0.049804688 to 0.59765625
- permitted_machine_sets: int32 [65536, 4], P(('node', 'local')), may hold values from 0 to 63, all different within a row; in each aligned block of 128 rows (0 to 127, 128 to 255, ...) at most 12 rows name the same one
- chosen_machine_specialist_tuples: int32 [65536, 8], P(('node', 'local')), may hold values from 0 to 31, as said below
- quota_per_class: int32 [512], P('node'), may hold values from 24 to 48, as said below
- gating_matrix_tensor: bfloat16 [512, 1024, 512], P(('node', 'local')), may hold values from -0.1875 to 0.1875
- widening_matrix_tensor: bfloat16 [512, 1024, 512], P(('node', 'local')), may hold values from -0.1875 to 0.1875
- shrinking_matrix_tensor: bfloat16 [512, 512, 1024], P(('node', 'local')), may hold values from -0.25 to 0.25
Outputs:
- mixed: bfloat16 [65536, 1024], P(('node', 'local'))
- input_grad: bfloat16 [65536, 1024], P(('node', 'local'))
- coefficient_derivative: bfloat16 [65536, 8], P(('node', 'local'))
Inputs may be any that keep to these rules, and one draw needn't show every extreme that they name: `permitted_machine_sets`: each row names 4 different node groups; in each aligned block of 128 rows (the rows of one device) no group is named by more than 12 rows. `chosen_machine_specialist_tuples`: each row holds 8 different numbers; number c picks position c // 8 of the token's permitted_machine_sets row and expert c mod 8 of that group; each of the 4 positions is picked at least once. `quota_per_class`: each a multiple of 8.
All inputs are finite; a program needn't handle non-finite values.
Results may differ from a plain program's by a relative error of at most 0.018.
Values may be sent and summed in bfloat16 or wider, within the bound.
A program may use at most 64 MiB of HBM per device.

v0:
```python
import jax
import jax.numpy as jnp
from jax import lax
from jax.sharding import PartitionSpec as P


def activations(row_block, weight_gate, weight_up):
    gate_act = jnp.dot(row_block, weight_gate, preferred_element_type=jnp.float32)
    up_act = jnp.dot(row_block, weight_up, preferred_element_type=jnp.float32)
    return (gate_act, up_act)


def expert_outputs(gate_act, up_act, weight_down):
    sigmoid_act = jax.nn.sigmoid(gate_act)
    hidden = (gate_act * sigmoid_act * up_act).astype(jnp.bfloat16)
    return jnp.dot(hidden, weight_down, preferred_element_type=jnp.float32).astype(jnp.bfloat16)


def contract_last(left_side, right_side):
    return lax.dot_general(
        left_side, right_side, (((1,), (1,)), ((), ())), preferred_element_type=jnp.float32
    )


def expert_grads(
    gate_act, up_act, outputs, gate_vals, upstream, weight_gate, weight_up, weight_down
):
    sigmoid_act = jax.nn.sigmoid(gate_act)
    back_prop = gate_vals.astype(jnp.float32)[:, None] * contract_last(upstream, weight_down)
    grad_gate = (back_prop * up_act * sigmoid_act * (1.0 + gate_act * (1.0 - sigmoid_act))).astype(
        jnp.bfloat16
    )
    grad_up = (back_prop * gate_act * sigmoid_act).astype(jnp.bfloat16)
    grad_rows = (contract_last(grad_gate, weight_gate) + contract_last(grad_up, weight_up)).astype(
        jnp.bfloat16
    )
    grad_weight = jnp.sum(
        upstream.astype(jnp.float32) * outputs.astype(jnp.float32), axis=1
    ).astype(jnp.bfloat16)
    return (grad_rows, grad_weight)


def pad_rows(matrix):
    return jnp.concatenate([matrix, jnp.zeros((1, matrix.shape[1]), matrix.dtype)], axis=0)


def route_plan(
    permitted_machine_sets,
    chosen_machine_specialist_tuples,
    dispatch_mixing_factors,
    node_count,
    local_count,
    group_slots,
):
    tok_rows, group_count = permitted_machine_sets.shape
    code_count = group_count * local_count
    matches = (
        chosen_machine_specialist_tuples[:, :, None]
        == jnp.arange(code_count, dtype=jnp.int32)[None, None, :]
    )
    gate_table = jnp.sum(
        jnp.where(matches, dispatch_mixing_factors[:, :, None].astype(jnp.float32), 0.0), axis=1
    )
    gate_table = gate_table.astype(jnp.bfloat16).reshape(tok_rows * group_count, local_count)
    flat_group = permitted_machine_sets.reshape(-1)
    onehot = (flat_group[:, None] == jnp.arange(node_count, dtype=jnp.int32)[None, :]).astype(
        jnp.int32
    )
    position = jnp.sum((jnp.cumsum(onehot, axis=0) - onehot) * onehot, axis=1)
    landing = flat_group * group_slots + position
    entries = tok_rows * group_count
    sender = (
        jnp.full((node_count * group_slots,), entries, jnp.int32)
        .at[landing]
        .set(jnp.arange(entries, dtype=jnp.int32))
    )
    return (gate_table, landing, sender)


def specialist_choice_map(arriving_gating_factors, quota_per_class, ordinal_under_quota):
    capacity_slot_count = arriving_gating_factors.shape[0] * arriving_gating_factors.shape[1]
    local_count = arriving_gating_factors.shape[2]
    flattened = arriving_gating_factors.reshape(capacity_slot_count, local_count)
    elected_members = (flattened != 0).astype(jnp.int32)
    sorting_place = jnp.cumsum(elected_members, axis=0) - elected_members
    accepted_booleans = (elected_members > 0) & (sorting_place < quota_per_class[None, :])
    resident_line = jnp.arange(local_count, dtype=jnp.int32)[None, :]
    discard_entry = local_count * ordinal_under_quota
    target = jnp.where(
        accepted_booleans, resident_line * ordinal_under_quota + sorting_place, discard_entry
    )
    slot_ids = jnp.broadcast_to(
        jnp.arange(capacity_slot_count, dtype=jnp.int32)[:, None],
        (capacity_slot_count, local_count),
    )
    token_provenance = (
        jnp.full((discard_entry + 1,), capacity_slot_count, jnp.int32)
        .at[target.reshape(-1)]
        .set(slot_ids.reshape(-1))[:discard_entry]
    )
    token_provenance = token_provenance.reshape(local_count, ordinal_under_quota)
    padded = pad_rows(flattened)
    expert_gate_values = padded[token_provenance, jnp.arange(local_count, dtype=jnp.int32)[:, None]]
    return (token_provenance, expert_gate_values, capacity_slot_count)


def slot_sums(terms, token_provenance, capacity_slot_count):
    feature = terms.shape[-1]
    summed = jax.ops.segment_sum(
        terms.reshape(-1, feature),
        token_provenance.reshape(-1),
        num_segments=capacity_slot_count + 1,
    )
    return summed[:capacity_slot_count].astype(jnp.bfloat16)


def slot_table(values, token_provenance, capacity_slot_count):
    local_count = token_provenance.shape[0]
    column = jnp.broadcast_to(
        jnp.arange(local_count, dtype=jnp.int32)[:, None], token_provenance.shape
    )
    table_out = jnp.zeros((capacity_slot_count + 1, local_count), values.dtype)
    table_out = table_out.at[token_provenance.reshape(-1), column.reshape(-1)].set(
        values.reshape(-1)
    )
    return table_out[:capacity_slot_count]


def token_sum(returned, landing, tok_rows):
    feature = returned.shape[-1]
    picked = returned.reshape(-1, feature)[landing].astype(jnp.float32)
    return jnp.sum(picked.reshape(tok_rows, -1, feature), axis=1).astype(jnp.bfloat16)


def token_grads(returned, landing, chosen_machine_specialist_tuples):
    local_count = returned.shape[-1]
    tok_rows = chosen_machine_specialist_tuples.shape[0]
    picked = returned.reshape(-1, local_count)[landing].reshape(tok_rows, -1)
    return jnp.take_along_axis(picked, chosen_machine_specialist_tuples, axis=1)


def per_device(
    input_activation_matrix,
    output_adjoint,
    dispatch_mixing_factors,
    permitted_machine_sets,
    chosen_machine_specialist_tuples,
    quota_per_class,
    gating_matrix_tensor,
    widening_matrix_tensor,
    shrinking_matrix_tensor,
):
    node_count = lax.axis_size("node")
    local_count = lax.axis_size("local")
    tok_rows, feature = input_activation_matrix.shape
    top_count = chosen_machine_specialist_tuples.shape[1]
    group_count = permitted_machine_sets.shape[1]
    group_slots = 3 * tok_rows * group_count // (2 * node_count)
    ordinal_under_quota = 6 * (tok_rows * top_count // (16 * local_count))
    weight_gate = gating_matrix_tensor[0]
    weight_up = widening_matrix_tensor[0]
    weight_down = shrinking_matrix_tensor[0]
    gate_table, landing, sender = route_plan(
        permitted_machine_sets,
        chosen_machine_specialist_tuples,
        dispatch_mixing_factors,
        node_count,
        local_count,
        group_slots,
    )
    token_of = sender // group_count
    send_rows = pad_rows(input_activation_matrix)[token_of].reshape(
        node_count, group_slots, feature
    )
    send_up = pad_rows(output_adjoint)[token_of].reshape(node_count, group_slots, feature)
    send_gates = pad_rows(gate_table)[sender].reshape(node_count, group_slots, local_count)
    recv_rows, arriving_gating_factors = (
        lax.all_to_all(send_rows, "node", split_axis=0, concat_axis=0, tiled=True),
        lax.all_to_all(send_gates, "node", split_axis=0, concat_axis=0, tiled=True),
    )
    token_provenance, expert_gate_values, capacity_slot_count = specialist_choice_map(
        arriving_gating_factors, quota_per_class, ordinal_under_quota
    )
    out_rows = pad_rows(recv_rows.reshape(capacity_slot_count, feature))[token_provenance]
    in_rows, in_gates = (
        lax.all_to_all(out_rows, "local", split_axis=0, concat_axis=0, tiled=True),
        lax.all_to_all(expert_gate_values, "local", split_axis=0, concat_axis=0, tiled=True),
    )
    gate_act, up_act = activations(in_rows.reshape(-1, feature), weight_gate, weight_up)
    outputs = expert_outputs(gate_act, up_act, weight_down)
    out_back = lax.all_to_all(
        outputs.reshape(local_count, ordinal_under_quota, feature),
        "local",
        split_axis=0,
        concat_axis=0,
        tiled=True,
    )
    mix_part = slot_sums(
        expert_gate_values.astype(jnp.float32)[:, :, None] * out_back.astype(jnp.float32),
        token_provenance,
        capacity_slot_count,
    )
    mix_home = lax.all_to_all(
        mix_part.reshape(node_count, group_slots, feature),
        "node",
        split_axis=0,
        concat_axis=0,
        tiled=True,
    )
    recv_up = lax.all_to_all(send_up, "node", split_axis=0, concat_axis=0, tiled=True)
    out_up = pad_rows(recv_up.reshape(capacity_slot_count, feature))[token_provenance]
    in_up = lax.all_to_all(out_up, "local", split_axis=0, concat_axis=0, tiled=True)
    grad_rows, grad_weight = expert_grads(
        gate_act,
        up_act,
        outputs,
        in_gates.reshape(-1),
        in_up.reshape(-1, feature),
        weight_gate,
        weight_up,
        weight_down,
    )
    grad_back, weight_back = (
        lax.all_to_all(
            grad_rows.reshape(local_count, ordinal_under_quota, feature),
            "local",
            split_axis=0,
            concat_axis=0,
            tiled=True,
        ),
        lax.all_to_all(
            grad_weight.reshape(local_count, ordinal_under_quota),
            "local",
            split_axis=0,
            concat_axis=0,
            tiled=True,
        ),
    )
    grad_part = slot_sums(grad_back.astype(jnp.float32), token_provenance, capacity_slot_count)
    weight_part = slot_table(weight_back, token_provenance, capacity_slot_count)
    grad_home, weight_home = (
        lax.all_to_all(
            grad_part.reshape(node_count, group_slots, feature),
            "node",
            split_axis=0,
            concat_axis=0,
            tiled=True,
        ),
        lax.all_to_all(
            weight_part.reshape(node_count, group_slots, local_count),
            "node",
            split_axis=0,
            concat_axis=0,
            tiled=True,
        ),
    )
    mixed = token_sum(mix_home, landing, tok_rows)
    input_grad = token_sum(grad_home, landing, tok_rows)
    coefficient_derivative = token_grads(weight_home, landing, chosen_machine_specialist_tuples)
    return (mixed, input_grad, coefficient_derivative)


def solution(mesh):
    return jax.shard_map(
        per_device,
        mesh=mesh,
        in_specs=(
            P(("node", "local"), None),
            P(("node", "local"), None),
            P(("node", "local"), None),
            P(("node", "local"), None),
            P(("node", "local"), None),
            P("node"),
            P(("node", "local"), None, None),
            P(("node", "local"), None, None),
            P(("node", "local"), None, None),
        ),
        out_specs=(
            P(("node", "local"), None),
            P(("node", "local"), None),
            P(("node", "local"), None),
        ),
        check_vma=False,
    )
```

profile of v0, /device:TPU:6, one launch (start us, length us, event | category | flops | bytes accessed | tf_op | source)
XLA Modules:
  0.0 444.4 jit_solution(1862005547645688031)
XLA Ops:
  4.3 1.2 reduce-window.14
  5.9 2.4 scatter_custom_fusion
  8.5 1.9 gather_fusion
  11.5 13.8 %all-to-all-start = ((bf16[64,12,8]{1,2,0:T(8,128)(2,1)}), bf16[64,12,8]{1,2,0:T(8,128)(2,1)S(1)}, u32[]{:S(2)}, u32[]{:S(2)}) async-start(bf16[64,12,8]{1,2,0:T(8,128)(2,1)} %copy.88), calls=%async_computation | async-start | bytes 262144 | tf_op jit(solution)/shard_map/all_to_all | solution.py:179
  25.4 2.8 gather_fusion.2
  28.2 1.5 reshape.286
  29.7 4.8 %all-to-all-done = bf16[64,12,8]{1,2,0:T(8,128)(2,1)S(1)} async-done(((bf16[64,12,8]{1,2,0:T(8,128)(2,1)}), bf16[64,12,8]{1,2,0:T(8,128)(2,1)S(1)}, u32[]{:S(2)}, u32[]{:S(2)}) %all-to-all-start) | async-done | bytes 12320 | tf_op jit(solution)/shard_map/all_to_all | solution.py:179
  35.1 6.5 %all-to-all-start.1 = ((bf16[64,12,1024]{2,1,0:T(8,128)(2,1)}), bf16[64,12,1024]{2,1,0:T(8,128)(2,1)S(1)}, u32[]{:S(2)}, u32[]{:S(2)}) async-start(bf16[64,12,1024]{2,1,0:T(8,128)(2,1)} %reshape.286), calls=%async_computation.1 | async-start | bytes 4194304 | tf_op jit(solution)/shard_map/all_to_all | solution.py:178
  41.7 1.0 concatenate.29
  42.6 3.6 gather_fusion.5
  46.2 3.6 reshape.293
  49.8 43.2 %all-to-all-done.1 = bf16[64,12,1024]{2,1,0:T(8,128)(2,1)S(1)} async-done(((bf16[64,12,1024]{2,1,0:T(8,128)(2,1)}), bf16[64,12,1024]{2,1,0:T(8,128)(2,1)S(1)}, u32[]{:S(2)}, u32[]{:S(2)}) %all-to-all-start.1) | async-done | bytes 1572896 | tf_op jit(solution)/shard_map/all_to_all | solution.py:178
  93.0 5.6 %all-to-all-start.6 = ((bf16[64,12,1024]{2,1,0:T(8,128)(2,1)}), bf16[64,12,1024]{2,1,0:T(8,128)(2,1)}, u32[]{:S(2)}, u32[]{:S(2)}) async-start(bf16[64,12,1024]{2,1,0:T(8,128)(2,1)} %reshape.293), calls=%async_computation.6 | async-start | bytes 4194304 | tf_op jit(solution)/shard_map/all_to_all | solution.py:210
  100.6 1.7 reduce-window.16
  102.8 1.3 add_select_fusion
  106.6 23.1 %scatter_custom_fusion.1 = s32[385]{0:T(512)S(1)} fusion(s32[6144]{0:T(1024)S(1)} %bitcast.90, s32[6144]{0:T(1024)} %reshape.398, s32[]{:T(128)} %constant.23.clone.1), kind=kCustom, calls=%fused_computation.90 | custom fusion | bytes 2052 | tf_op jit(solution)/shard_map/scatter | solution.py:99
  130.0 1.4 reshape.287
  131.4 1.5 concatenate.28
  132.9 2.7 gather_fusion.3
  135.6 14.3 %all-to-all-done.6 = bf16[64,12,1024]{2,1,0:T(8,128)(2,1)} async-done(((bf16[64,12,1024]{2,1,0:T(8,128)(2,1)}), bf16[64,12,1024]{2,1,0:T(8,128)(2,1)}, u32[]{:S(2)}, u32[]{:S(2)}) %all-to-all-start.6) | async-done | bytes 1572896 | tf_op jit(solution)/shard_map/all_to_all | solution.py:210
  149.9 7.1 %all-to-all-start.2 = ((bf16[8,48,1024]{2,1,0:T(8,128)(2,1)}), bf16[8,48,1024]{2,1,0:T(8,128)(2,1)S(1)}, u32[]{:S(2)}, u32[]{:S(2)}) async-start(bf16[8,48,1024]{2,1,0:T(8,128)(2,1)} %bitcast.85), calls=%async_computation.2 | async-start | bytes 1572864 | tf_op jit(solution)/shard_map/all_to_all | solution.py:186
  157.0 3.6 reshape.294
  160.6 1.5 concatenate.30
  162.1 2.7 gather_fusion.6
  164.8 13.9 %all-to-all-done.2 = bf16[8,48,1024]{2,1,0:T(8,128)(2,1)S(1)} async-done(((bf16[8,48,1024]{2,1,0:T(8,128)(2,1)}), bf16[8,48,1024]{2,1,0:T(8,128)(2,1)S(1)}, u32[]{:S(2)}, u32[]{:S(2)}) %all-to-all-start.2) | async-done | bytes 786464 | tf_op jit(solution)/shard_map/all_to_all | solution.py:186
  178.7 3.5 all-to-all-start.7
  182.3 2.8 fusion.12
  185.1 1.5 fusion.8
  186.5 17.3 %all-to-all-done.7 = bf16[8,48,1024]{2,1,0:T(8,128)(2,1)S(1)} async-done(((bf16[8,48,1024]{2,1,0:T(8,128)(2,1)}), bf16[8,48,1024]{2,1,0:T(8,128)(2,1)S(1)}, u32[]{:S(2)}, u32[]{:S(2)}) %all-to-all-start.7) | async-done | bytes 786464 | tf_op jit(solution)/shard_map/all_to_all | solution.py:212
  203.9 2.9 multiply_reduce_fusion
  207.4 3.3 all-to-all-start.10
  211.2 3.6 gather_fusion.1
  215.5 2.8 all-to-all-done.10
  218.3 4.3 all-to-all-start.5
  222.8 20.1 %scatter_fusion = bf16[769,8]{0,1:T(8,128)(2,1)S(1)} fusion(bf16[769,8]{0,1:T(8,128)(2,1)S(1)} %broadcast_in_dim.46, s32[384]{0:T(512)S(1)} %fusion.27, bf16[384]{0:T(512)(128)(2,1)S(1)} %reshape.420), kind=kCustom, calls=%fused_computation.14 | custom fusion | bytes 5376 | tf_op jit(solution)/shard_map/scatter | solution.py:123
  243.3 17.6 %all_to_all.66 = bf16[64,12,8]{1,2,0:T(8,128)(2,1)S(1)} all-to-all(bf16[64,12,8]{1,2,0:T(8,128)(2,1)S(1)} %copy.96), channel_id=1, replica_groups=mesh['node'=64,'local'=8] {'node'}, dimensions={0} | all-to-all | bytes 24576 | tf_op jit(solution)/shard_map/all_to_all | solution.py:249
  260.9 7.2 %all-to-all-start.3 = ((bf16[8,48,1024]{2,1,0:T(8,128)(2,1)}), bf16[8,48,1024]{2,1,0:T(8,128)(2,1)S(1)}, u32[]{:S(2)}, u32[]{:S(2)}) async-start(bf16[8,48,1024]{2,1,0:T(8,128)(2,1)} %bitcast.89), calls=%async_computation.3 | async-start | bytes 1572864 | tf_op jit(solution)/shard_map/all_to_all | solution.py:191
  269.4 2.3 fusion.10
  271.8 1.5 add_convert_fusion
  273.3 17.8 %all-to-all-done.3 = bf16[8,48,1024]{2,1,0:T(8,128)(2,1)S(1)} async-done(((bf16[8,48,1024]{2,1,0:T(8,128)(2,1)}), bf16[8,48,1024]{2,1,0:T(8,128)(2,1)S(1)}, u32[]{:S(2)}, u32[]{:S(2)}) %all-to-all-start.3) | async-done | bytes 786464 | tf_op jit(solution)/shard_map/all_to_all | solution.py:191
  291.1 4.2 all-to-all-start.8
  295.4 1.3 convert_multiply_fusion
  296.7 6.3 %scatter_custom_fusion.2 = f32[769,1024]{1,0:T(8,128)} fusion(s32[384]{0:T(512)S(1)} %get-tuple-element.17, f32[384,1024]{1,0:T(8,128)} %bitcast.88, f32[]{:T(128)} %constant.22.clone.1), kind=kCustom, calls=%fused_computation.19 | custom fusion | flops 393216 | bytes 3150336 | tf_op jit(solution)/shard_map/scatter-add | solution.py:109
  303.0 2.1 slice.66
  305.1 1.6 reshape.291
  306.7 12.2 %all-to-all-done.8 = bf16[8,48,1024]{2,1,0:T(8,128)(2,1)} async-done(((bf16[8,48,1024]{2,1,0:T(8,128)(2,1)}), bf16[8,48,1024]{2,1,0:T(8,128)(2,1)}, u32[]{:S(2)}, u32[]{:S(2)}) %all-to-all-start.8) | async-done | bytes 786464 | tf_op jit(solution)/shard_map/all_to_all | solution.py:224
  318.9 7.2 %all-to-all-start.4 = ((bf16[64,12,1024]{2,1,0:T(8,128)(2,1)}), bf16[64,12,1024]{2,1,0:T(8,128)(2,1)S(1)}, u32[]{:S(2)}, u32[]{:S(2)}) async-start(bf16[64,12,1024]{2,1,0:T(8,128)(2,1)} %reshape.291), calls=%async_computation.4 | async-start | bytes 4194304 | tf_op jit(solution)/shard_map/all_to_all | solution.py:203
  326.1 6.2 %scatter_custom_fusion.3 = f32[769,1024]{1,0:T(8,128)} fusion(s32[384]{0:T(512)S(1)} %get-tuple-element.17, f32[]{:T(128)} %constant.22.clone.1, bf16[384,1024]{1,0:T(8,128)(2,1)} %bitcast.23), kind=kCustom, calls=%fused_computation.17 | custom fusion | flops 786432 | bytes 3936260 | tf_op jit(solution)/shard_map/scatter-add | solution.py:109
  332.2 3.4 slice.65
  335.6 3.6 reshape.299
  339.2 38.3 %all-to-all-done.4 = bf16[64,12,1024]{2,1,0:T(8,128)(2,1)S(1)} async-done(((bf16[64,12,1024]{2,1,0:T(8,128)(2,1)}), bf16[64,12,1024]{2,1,0:T(8,128)(2,1)S(1)}, u32[]{:S(2)}, u32[]{:S(2)}) %all-to-all-start.4) | async-done | bytes 1572896 | tf_op jit(solution)/shard_map/all_to_all | solution.py:203
  377.4 1.3 copy-done.1
  378.8 5.6 %all-to-all-start.9 = ((bf16[64,12,1024]{2,1,0:T(8,128)(2,1)}), bf16[64,12,1024]{2,1,0:T(8,128)(2,1)}, u32[]{:S(2)}, u32[]{:S(2)}) async-start(bf16[64,12,1024]{2,1,0:T(8,128)(2,1)} %reshape.299), calls=%async_computation.9 | async-start | bytes 4194304 | tf_op jit(solution)/shard_map/all_to_all | solution.py:242
  385.0 1.3 gather_fusion.8
  386.5 9.0 %gather_fusion.9 = bf16[1024]{0:T(1024)(128)(2,1)S(1)} fusion(bf16[128,32]{1,0:T(8,128)(2,1)S(1)} %reshape.305, s32[1024]{0:T(1024)S(1)} %reshape.380), kind=kCustom, calls=%fused_computation.9 | custom fusion | bytes 12288 | tf_op jit(solution)/shard_map/jit(take_along_axis)/gather | solution.py:139
  396.3 2.5 reshape.292
  398.8 2.8 gather_fusion.4
  401.6 1.5 gather.40
  403.0 2.1 reduce_sum.56
  405.1 30.4 %all-to-all-done.9 = bf16[64,12,1024]{2,1,0:T(8,128)(2,1)} async-done(((bf16[64,12,1024]{2,1,0:T(8,128)(2,1)}), bf16[64,12,1024]{2,1,0:T(8,128)(2,1)}, u32[]{:S(2)}, u32[]{:S(2)}) %all-to-all-start.9) | async-done | bytes 1572896 | tf_op jit(solution)/shard_map/all_to_all | solution.py:242
  435.6 2.5 reshape.300
  438.1 2.8 gather_fusion.7
  440.9 1.5 gather.44
  442.3 2.1 reduce_sum.57
  (89 shorter events, 16.2 us)
Async XLA Ops:
  0.6 203.2 %copy-start = (bf16[1,512,1024]{2,1,0:T(8,128)(2,1)S(1)}, bf16[1,512,1024]{2,1,0:T(8,128)(2,1)}, u32[]{:S(2)}) copy-start(bf16[1,512,1024]{2,1,0:T(8,128)(2,1)} %param.17) | copy-start | bytes 3145732
  5.7 19.6 %copy-start.7 = (bf16[128,1024]{1,0:T(8,128)(2,1)S(1)}, bf16[128,1024]{1,0:T(8,128)(2,1)}, u32[]{:S(2)}) copy-start(bf16[128,1024]{1,0:T(8,128)(2,1)} %param.9) | copy-start | bytes 786436
  11.5 23.0 %all-to-all-start = ((bf16[64,12,8]{1,2,0:T(8,128)(2,1)}), bf16[64,12,8]{1,2,0:T(8,128)(2,1)S(1)}, u32[]{:S(2)}, u32[]{:S(2)}) async-start(bf16[64,12,8]{1,2,0:T(8,128)(2,1)} %copy.88), calls=%async_computation | async-start | bytes 262144 | tf_op jit(solution)/shard_map/all_to_all | solution.py:179
  34.5 0.7 copy-start.6
  35.1 57.9 %all-to-all-start.1 = ((bf16[64,12,1024]{2,1,0:T(8,128)(2,1)}), bf16[64,12,1024]{2,1,0:T(8,128)(2,1)S(1)}, u32[]{:S(2)}, u32[]{:S(2)}) async-start(bf16[64,12,1024]{2,1,0:T(8,128)(2,1)} %reshape.286), calls=%async_computation.1 | async-start | bytes 4194304 | tf_op jit(solution)/shard_map/all_to_all | solution.py:178
  93.0 56.8 %all-to-all-start.6 = ((bf16[64,12,1024]{2,1,0:T(8,128)(2,1)}), bf16[64,12,1024]{2,1,0:T(8,128)(2,1)}, u32[]{:S(2)}, u32[]{:S(2)}) async-start(bf16[64,12,1024]{2,1,0:T(8,128)(2,1)} %reshape.293), calls=%async_computation.6 | async-start | bytes 4194304 | tf_op jit(solution)/shard_map/all_to_all | solution.py:210
  149.9 28.9 %all-to-all-start.2 = ((bf16[8,48,1024]{2,1,0:T(8,128)(2,1)}), bf16[8,48,1024]{2,1,0:T(8,128)(2,1)S(1)}, u32[]{:S(2)}, u32[]{:S(2)}) async-start(bf16[8,48,1024]{2,1,0:T(8,128)(2,1)} %bitcast.85), calls=%async_computation.2 | async-start | bytes 1572864 | tf_op jit(solution)/shard_map/all_to_all | solution.py:186
  178.7 25.1 %all-to-all-start.7 = ((bf16[8,48,1024]{2,1,0:T(8,128)(2,1)}), bf16[8,48,1024]{2,1,0:T(8,128)(2,1)S(1)}, u32[]{:S(2)}, u32[]{:S(2)}) async-start(bf16[8,48,1024]{2,1,0:T(8,128)(2,1)} %bitcast.86), calls=%async_computation.7 | async-start | bytes 1572864 | tf_op jit(solution)/shard_map/all_to_all | solution.py:212
  182.3 2.8 copy-start.3
  207.4 10.8 %all-to-all-start.10 = ((bf16[8,1,48]{2,1,0:T(2,128)(2,1)}), bf16[8,1,48]{2,1,0:T(2,128)(2,1)S(1)}, u32[]{:S(2)}, u32[]{:S(2)}) async-start(bf16[8,1,48]{2,1,0:T(2,128)(2,1)} %convert_element_type.106), calls=%async_computation.10 | async-start | bytes 8192 | tf_op jit(solution)/shard_map/all_to_all | solution.py:231
  218.3 25.0 %all-to-all-start.5 = ((bf16[8,1,48]{2,1,0:T(2,128)(2,1)}), bf16[8,1,48]{2,1,0:T(2,128)(2,1)S(1)}, u32[]{:S(2)}, u32[]{:S(2)}) async-start(bf16[8,1,48]{2,1,0:T(2,128)(2,1)} %all_to_all.53), calls=%async_computation.5 | async-start | bytes 8192 | tf_op jit(solution)/shard_map/all_to_all | solution.py:187
  260.9 30.2 %all-to-all-start.3 = ((bf16[8,48,1024]{2,1,0:T(8,128)(2,1)}), bf16[8,48,1024]{2,1,0:T(8,128)(2,1)S(1)}, u32[]{:S(2)}, u32[]{:S(2)}) async-start(bf16[8,48,1024]{2,1,0:T(8,128)(2,1)} %bitcast.89), calls=%async_computation.3 | async-start | bytes 1572864 | tf_op jit(solution)/shard_map/all_to_all | solution.py:191
  268.2 1.2 copy-start.2
  269.4 2.3 copy-start.4
  269.4 2.3 copy-start.5
  291.1 27.8 %all-to-all-start.8 = ((bf16[8,48,1024]{2,1,0:T(8,128)(2,1)}), bf16[8,48,1024]{2,1,0:T(8,128)(2,1)}, u32[]{:S(2)}, u32[]{:S(2)}) async-start(bf16[8,48,1024]{2,1,0:T(8,128)(2,1)} %bitcast.18), calls=%async_computation.8 | async-start | bytes 1572864 | tf_op jit(solution)/shard_map/all_to_all | solution.py:224
  318.9 58.5 %all-to-all-start.4 = ((bf16[64,12,1024]{2,1,0:T(8,128)(2,1)}), bf16[64,12,1024]{2,1,0:T(8,128)(2,1)S(1)}, u32[]{:S(2)}, u32[]{:S(2)}) async-start(bf16[64,12,1024]{2,1,0:T(8,128)(2,1)} %reshape.291), calls=%async_computation.4 | async-start | bytes 4194304 | tf_op jit(solution)/shard_map/all_to_all | solution.py:203
  339.2 45.2 %copy-start.8 = (s32[128,8]{0,1:T(8,128)S(1)}, s32[128,8]{0,1:T(8,128)}, u32[]{:S(2)}) copy-start(s32[128,8]{0,1:T(8,128)} %param.13) | copy-start | bytes 12292
  377.4 1.3 copy-start.1
  378.8 56.8 %all-to-all-start.9 = ((bf16[64,12,1024]{2,1,0:T(8,128)(2,1)}), bf16[64,12,1024]{2,1,0:T(8,128)(2,1)}, u32[]{:S(2)}, u32[]{:S(2)}) async-start(bf16[64,12,1024]{2,1,0:T(8,128)(2,1)} %reshape.299), calls=%async_computation.9 | async-start | bytes 4194304 | tf_op jit(solution)/shard_map/all_to_all | solution.py:242
where the time goes:
time: 446 us; the launch traced here: 444 us
  waiting for transfers between devices  195 us (44%)
  local copies, waits for them, and re-layouts  124 us (28%)
  starting transfers between devices  68.3 us (15%)
  other arithmetic  26.3 us (6%)
  blocking collectives  17.6 us (4%)
  matrix products  11.6 us (3%)
    all_to_all x1, waiting for transfers between devices, per_device(): lax.all_to_all(send_rows, 'node', split_axis=0, concat_axis=0, tiled=True)  43.2 us
    all_to_all x1, waiting for transfers between devices, per_device(): lax.all_to_all(mix_part.reshape(node_count, group_slots, feature), 'node'...  38.3 us
    all_to_all x1, waiting for transfers between devices, per_device(): lax.all_to_all(grad_part.reshape(node_count, group_slots, feature), 'node...  30.4 us
    scatter x1, local copies, waits for them, and re-layouts, specialist_choice_map(): token_provenance = jnp.full((discard_entry + 1,), capacity_slot_count, jn...  23.1 us
    scatter x1, local copies, waits for them, and re-layouts, slot_table(): table_out.at[token_provenance.reshape(-1), column.reshape(-1)]  20.1 us
    all_to_all x1, waiting for transfers between devices, per_device(): lax.all_to_all(outputs.reshape(local_count, ordinal_under_quota, feature)...  17.8 us
    all_to_all x1, blocking collectives, per_device(): lax.all_to_all(weight_part.reshape(node_count, group_slots, local_count),...  17.6 us
    all_to_all x1, waiting for transfers between devices, per_device(): lax.all_to_all(out_up, 'local', split_axis=0, concat_axis=0, tiled=True)  17.3 us
  transfers between devices with their start and end apart: 11, of which 10 were waited for; matrix products, arithmetic and copies ran while one was open for 31% of the time, Pallas kernels for 0%

commit v1 on v0

v1 whole, which is shorter than its diff:
```python
import functools
import math
from types import SimpleNamespace

import jax
import jax.numpy as jnp
from jax import lax
from jax.experimental import pallas as pl
from jax.experimental.pallas import tpu as pltpu
from jax.sharding import PartitionSpec as P

MESH = pl.DeviceIdType.MESH
BF = jnp.bfloat16
F32 = jnp.float32


def config(mesh, tok, kg, top, feature, hidden, most=12, quota=48):
    c = SimpleNamespace()
    c.NN, c.NL = mesh.shape["node"], mesh.shape["local"]
    c.NK, c.NX = (2, 8) if c.NN == 64 else (1, 4)
    c.NZ = c.NN // (c.NK * c.NX)
    c.NQ = c.NZ * c.NK
    c.PC = c.NX // 2
    c.D2 = c.NX // 2
    c.NH = c.NX - 1
    c.TOK, c.KG, c.TOP, c.D, c.F = tok, kg, top, feature, hidden
    c.J, c.Q = most, quota
    c.NC = 2
    c.W = feature // c.NC
    c.NS = 2 * c.NC
    c.BL = c.PC * c.J
    c.I = 2 * c.NQ * c.BL
    c.R = c.NL * c.Q
    c.H = tok // 2
    return c


def ring_steps(c):
    right, left = [], []
    for d in range(1, c.D2):
        right += [(d, 0), (d, 1)]
        left += [(d, 1), (d, 0)]
    return right + [(c.D2, 0)], left + [(c.D2, 1)]


def slot_of(c, d, side):
    if d == 0:
        return 0
    return 2 * d - 1 if (side == 0 or d == c.D2) else 2 * d


def plan(c):
    NS, NC, NH = c.NS, c.NC, c.NH
    tx, tz, ty, lat = 1.4, 4.5, 9.0, 1.5
    tasks, links = {}, {}

    def add(key, pri, cost, deps, sends=()):
        tasks[key] = (pri, cost, deps, sends)

    add(("meta1",), -9, 1.5, [], [(("M1",), "x", 0.2)])
    add(("meta2",), -8, 0.5, [("M1",)], [(("M2",), "z", 0.2)])
    add(("pick",), -7, 1.5, [("M1",)])
    add(("rank",), -6, 2.0, [("M2",)])
    for s in range(NS):
        for h in range(NH):
            deps = [("AG", s, h - 2)] if h >= 2 else ([("ag", s - 1, NH - 3)] if s else [])
            add(("ag", s, h), s * 10 - 100, 0.1, deps, [(("AG", s, h), "x", tx)])
        for ch in range(2):
            need = 3 if ch == 0 and c.D2 > 2 else NH - 1
            deps = [("pick",)] + [("AG", s, g) for g in range(need + 1)]
            add(("z", s, ch), s * 10 + ch, 0.8, deps, [(("Z", s, ch), "z", tz)])
        add(("y", s), s * 10 + 3, 0.9, [("rank",), ("Z", s, 0), ("Z", s, 1)], [(("Y", s), "y", ty)])
    for s in range(NS):
        deps = [("Y", s)] + ([("e", s - 1)] if s else [])
        sends = []
        if s == NC - 1:
            sends = [(("B", u), "y", ty) for u in range(NC)]
        if s == NS - 1:
            sends = [(("B", u), "y", ty) for u in range(NC, NS)]
        add(("e", s), s * 10 + 4, 2.0, deps, sends)
        for ch in (1, 0):
            add(("m", s, ch), s * 10 + 5 - ch, 0.8, [("B", s)], [(("RZ", s, ch), "z", tz)])
            add(("p", s, ch), s * 10 + 7 - ch, 0.8, [("RZ", s, ch)])
        for h in range(NH):
            deps = [("p", s, 1)] + ([("p", s, 0)] if h > (2 if c.D2 > 2 else 0) else [])
            deps += [("RS", s, h - 2)] if h >= 2 else []
            add(("rs", s, h), s * 10 - 90, 0.15, deps, [(("RS", s, h), "x", tx)])
        add(("fin", s), s * 10 + 8, 0.3, [("p", s, 0), ("RS", s, NH - 1), ("RS", s, NH - 2)])
    add(("c1",), 45, 1.0, [("m", u, 0) for u in range(NC)] + [("y", u) for u in range(NC, NS)], [(("C1",), "z", 0.2)])
    add(("c2",), 46, 0.2, [("C1",)], [(("C2",), "x", 0.2)])
    add(("c3",), 47, 0.5, [("C2",)])

    done, now, order = {}, 0.0, []
    left = dict(tasks)
    while left:
        best = None
        for key, (pri, cost, deps, sends) in left.items():
            if any(d not in done for d in deps):
                continue
            at = max([done[d] for d in deps], default=0.0)
            rank = (max(at, now), pri, key)
            if best is None or rank < best[0]:
                best = (rank, key)
        key = best[1]
        pri, cost, deps, sends = left.pop(key)
        now = best[0][0] + cost
        done[key] = now
        for event, link, length in sends:
            start = max(now, links.get(link, 0.0))
            links[link] = start + length
            done[event] = start + length + lat
        order.append(key)
    return order, now


def iota(shape, dim):
    return lax.broadcasted_iota(jnp.int32, shape, dim)


def idiv(v, d):
    if d & (d - 1) == 0:
        return lax.shift_right_logical(v, jnp.int32(d.bit_length() - 1)) if d > 1 else v
    return ((v.astype(F32) + 0.5) * (1.0 / d)).astype(jnp.int32)


def imod(v, d):
    if d & (d - 1) == 0:
        return v & (d - 1)
    return v - idiv(v, d) * d


def onehot(mask):
    return jnp.where(mask, 1.0, 0.0).astype(BF)


def mm(a, b):
    return lax.dot_general(a, b, (((1,), (0,)), ((), ())), preferred_element_type=F32)


def mm_nt(a, b):
    return lax.dot_general(a, b, (((1,), (1,)), ((), ())), preferred_element_type=F32)


def kernel(c, order, x_ref, dy_ref, fac_ref, perm_ref, cho_ref, quota_ref, wg_hbm, wu_hbm, wd_hbm,
           mixed_ref, igrad_ref, coef_ref,
           wg, wu, wd, xg, zs, zr, ys, yr, bs, br, rzs, rzr, part, rss, rsr,
           pick, pickt, sel, selt, selg, ag, au, bk, meta, m1, m2s, m2, cm, c1r, c2s, c2r, acat, pmask,
           w_sem, s_small, r_small, ag_s, ag_r, z_s, z_r, y_s, y_r, b_s, b_r, rz_s, rz_r, rs_s, rs_r):
    NX, NQ, NL, PC, J, Q, TOK, NS, NC, W = c.NX, c.NQ, c.NL, c.PC, c.J, c.Q, c.TOK, c.NS, c.NC, c.W
    NG, I, R, BL = c.NN, c.I, c.R, c.BL
    LANES = 128
    node, y = lax.axis_index("node"), lax.axis_index("local")
    k, xx, zz = lax.rem(node, c.NK), lax.rem(lax.div(node, c.NK), NX), lax.div(node, c.NK * NX)
    b_me = zz * c.NK + k

    def x_peer(o):
        return (zz * NX + lax.rem(xx + (o + NX), NX)) * c.NK + k

    def q_peer(i):
        q = lax.rem(b_me + i, NQ)
        return q, (lax.div(q, c.NK) * NX + xx) * c.NK + lax.rem(q, c.NK)

    def y_peer(i):
        return lax.rem(y + i, NL)

    def copy(src, dst, send, recv, to_node, to_local):
        return pltpu.make_async_remote_copy(src_ref=src, dst_ref=dst, send_sem=send, recv_sem=recv,
                                            device_id=(to_node, to_local), device_id_type=MESH)

    def await_recv(like, sem):
        copy(like, like, sem, sem, node, y).wait_recv()

    def await_send(like, sem):
        copy(like, like, sem, sem, node, y).wait_send()

    barrier = pltpu.get_barrier_semaphore()
    for o in range(1, NX):
        pl.semaphore_signal(barrier, inc=1, device_id=(x_peer(o), y), device_id_type=MESH)
    for i in range(1, NQ):
        pl.semaphore_signal(barrier, inc=1, device_id=(q_peer(i)[1], y), device_id_type=MESH)
    for i in range(1, NL):
        pl.semaphore_signal(barrier, inc=1, device_id=(node, y_peer(i)), device_id_type=MESH)

    weights = [pltpu.make_async_copy(h.at[0], v, w_sem.at[n])
               for n, (h, v) in enumerate(((wg_hbm, wg), (wu_hbm, wu), (wd_hbm, wd)))]
    for w in weights:
        w.start()
    for s in range(NS):
        src = x_ref if s < NC else dy_ref
        xg[s, 0] = src[:, (s % NC) * W:(s % NC + 1) * W]
    pl.semaphore_wait(barrier, (NX - 1) + (NQ - 1) + (NL - 1))

    rights, lefts = ring_steps(c)

    def offset_of(p):
        d = lax.shift_right_logical(p + 1, jnp.int32(1))
        return jnp.where((p & 1) == 1, -d, d)

    def static_offset(p):
        d = (p + 1) // 2
        return -d if p % 2 else d

    def do_ag(s, h):
        for side, steps in ((0, rights), (1, lefts)):
            if h >= 2 and (s, h - 2) not in waited:
                d0, h0 = steps[h - 2]
                await_recv(xg.at[s, slot_of(c, d0, side), pl.ds(h0 * c.H, c.H)], ag_r.at[s, side, h - 2])
            d, half = steps[h]
            rows = pl.ds(half * c.H, c.H)
            copy(xg.at[s, slot_of(c, d - 1, side), rows], xg.at[s, slot_of(c, d, side), rows],
                 ag_s.at[s], ag_r.at[s, side, h], x_peer(1 if side == 0 else -1), y).start()

    ag_seen = {s: 0 for s in range(NS)}

    def ag_upto(s, h):
        for g in range(ag_seen[s], h + 1):
            if g + 2 >= c.NH or (("ag", s, g + 2) not in issued):
                for side, steps in ((0, rights), (1, lefts)):
                    d0, h0 = steps[g]
                    await_recv(xg.at[s, slot_of(c, d0, side), pl.ds(h0 * c.H, c.H)], ag_r.at[s, side, g])
                waited.add((s, g))
        ag_seen[s] = max(ag_seen[s], h + 1)

    issued, waited = set(), set()

    def do_meta1():
        perm, cho = perm_ref[...], cho_ref[...]
        fac = fac_ref[...].astype(F32)
        lane = iota((TOK, LANES), 1)
        code = iota((TOK, c.KG * NL), 1)
        table = jnp.zeros((TOK, c.KG * NL), F32)
        for n in range(c.TOP):
            table += jnp.where(cho[:, n:n + 1] == code, fac[:, n:n + 1], 0.0)
        table = table.astype(BF)
        groups = iota((TOK, NG), 1)
        named = []
        for s in range(c.KG):
            g = perm[:, s:s + 1]
            gx = imod(idiv(g, c.NK), NX)
            gq = idiv(g, c.NK * NX) * c.NK + imod(g, c.NK)
            named.append(jnp.where(gx * NQ + gq == groups, 1.0, 0.0))
        total = sum(named[1:], named[0]).astype(BF)
        lower = onehot(iota((TOK, TOK), 1) < iota((TOK, TOK), 0))
        place = mm(lower, total)
        mark = (iota((TOK, LANES), 0) + 1).astype(F32)
        lane_j = idiv(lane, NL)
        out = jnp.zeros((NG, LANES), F32)
        eye = onehot(iota((NG, NG), 0) == iota((NG, NG), 1))
        for s in range(c.KG):
            p = jnp.sum(named[s] * place, axis=1, keepdims=True).astype(jnp.int32)
            spread = onehot((iota((c.KG * NL, LANES), 0) == s * NL + imod(iota((c.KG * NL, LANES), 1), NL)))
            mine = (lane_j == p) & (lane < J * NL)
            rhs = jnp.where(mine, mm(table, spread), 0.0)
            rhs += jnp.where(lane - J * NL == p, mark, 0.0)
            a = named[s].astype(BF)
            out += mm(mm_nt(eye, a).astype(BF), rhs.astype(BF))
            acat[s] = a
            pmask[s] = onehot(mine)
        meta[...] = out.reshape(NX, NQ, LANES)
        m1[0] = meta[xx]
        for p in range(1, NX):
            to = lax.rem(xx + (NX - static_offset(p)), NX)
            copy(meta.at[to], m1.at[p], s_small.at[0], r_small.at[0], (zz * NX + to) * c.NK + k, y).start()

    def do_meta2():
        await_recv(m1.at[pl.ds(0, NX - 1)], r_small.at[0])
        flat = m1[...].reshape(NX * NQ, LANES).astype(BF)
        n = NX * NQ
        row, col = iota((n, n), 0), iota((n, n), 1)
        turn = onehot((imod(row, NX) == idiv(col, NQ)) & (idiv(row, NX) == imod(col, NQ)))
        m2s[...] = mm(turn, flat).reshape(NQ, NX, LANES)
        m2[b_me] = m2s[b_me]
        for i in range(1, NQ):
            q, to = q_peer(i)
            copy(m2s.at[q], m2.at[b_me], s_small.at[1], r_small.at[1], to, y).start()

    def do_pick():
        flat = m1[...].reshape(NX * NQ, LANES).astype(BF)
        C = NQ * BL
        row = iota((C, NX * NQ), 0)
        rq, rp = idiv(row, BL), idiv(imod(row, BL), J)
        lane, lrow = iota((C, LANES), 1), iota((C, LANES), 0)
        rcol = iota((C, 1), 0)
        ccol = iota((1, C), 1)
        for ch in range(2):
            take = onehot((rp + ch * PC) * NQ + rq == iota((C, NX * NQ), 1))
            got = jnp.where(lane == J * NL + imod(lrow, J), mm(take, flat), 0.0)
            down = jnp.sum(got, axis=1, keepdims=True).astype(jnp.int32)
            across = mm_nt(jnp.ones((8, LANES), BF), got.astype(BF))[0:1].astype(jnp.int32)
            down = jnp.where(down > 0, down + TOK * idiv(imod(rcol, BL), J), 0)
            across = jnp.where(across > 0, across + TOK * idiv(imod(ccol, BL), J), 0)
            pick[ch] = onehot(down == iota((C, PC * TOK), 1) + 1)
            pickt[ch] = onehot(across == iota((PC * TOK, C), 0) + 1)

    def slot_rows(v):
        half = NQ * BL
        ch = idiv(v, half)
        rest = v - ch * half
        return idiv(rest, BL) * NX + ch * PC + idiv(imod(rest, BL), J)

    def do_rank():
        await_recv(m2.at[pl.ds(0, NQ - 1)], r_small.at[1])
        n = NQ * NX
        mt = m2[...].reshape(n, LANES)
        lane = iota((n, LANES), 1)
        el = (mt != 0.0) & (lane < J * NL)
        elb = onehot(el)
        l0, l1 = iota((LANES, LANES), 0), iota((LANES, LANES), 1)
        same = (imod(l0, NL) == imod(l1, NL)) & (l0 < J * NL)
        inside = mm(elb, onehot(same & (idiv(l0, NL) < idiv(l1, NL))))
        rows = mm(elb, onehot(same)).astype(BF)

        def number(r):
            b, p = idiv(r, NX), imod(r, NX)
            return (idiv(b, c.NK) * NX + ((xx + offset_of(p) + NX) & (NX - 1))) * c.NK + imod(b, c.NK)

        before = onehot(number(iota((n, n), 1)) < number(iota((n, n), 0)))
        rank = inside + mm(before, rows)
        ql = jnp.broadcast_to(quota_ref[...].astype(F32), (8, NL)).astype(BF)
        ql = mm(ql, onehot(iota((NL, LANES), 0) == imod(iota((NL, LANES), 1), NL)))[0:1]
        keep = el & (rank < ql)
        rk = jnp.where(keep, rank + 1.0, 0.0).astype(BF)
        gk = jnp.where(keep, mt, 0.0).astype(BF)
        eye = onehot(l0 == l1)
        spread = onehot(iota((n, I), 0) == slot_rows(iota((n, I), 1)))
        mine = (idiv(iota((LANES, I), 0), NL) == imod(iota((LANES, I), 1), J)) & (iota((LANES, I), 0) < J * NL)
        fold = onehot((iota((max(NL, 8), LANES), 0) == imod(iota((max(NL, 8), LANES), 1), NL))
                      & (iota((max(NL, 8), LANES), 1) < J * NL))
        flat = jnp.where(mine, mm(mm_nt(eye, rk).astype(BF), spread), 0.0).astype(BF)
        flat = mm(fold, flat)
        for e in range(NL):
            sel[e] = onehot(flat[e:e + 1] == (iota((Q, I), 0) + 1).astype(F32))
        spread = onehot(slot_rows(iota((I, n), 0)) == iota((I, n), 1))
        mine = (idiv(iota((I, LANES), 1), NL) == imod(iota((I, LANES), 0), J)) & (iota((I, LANES), 1) < J * NL)
        widen = onehot((imod(iota((LANES, R), 0), NL) == idiv(iota((LANES, R), 1), Q)) & (iota((LANES, R), 0) < J * NL))
        flat = mm(jnp.where(mine, mm(spread, rk), 0.0).astype(BF), widen)
        gates = mm(jnp.where(mine, mm(spread, gk), 0.0).astype(BF), widen)
        hit = flat == (imod(iota((I, R), 1), Q) + 1).astype(F32)
        selt[...] = onehot(hit)
        selg[...] = jnp.where(hit, gates, 0.0).astype(BF)

    def do_z(s, ch):
        ag_upto(s, 3 if ch == 0 and c.D2 > 2 else c.NH - 1)
        rows = xg[s, ch * PC:(ch + 1) * PC].reshape(PC * TOK, W)
        zs[s, ch] = mm(pick[ch], rows).astype(BF).reshape(NQ, BL, W)
        for i in range(1, NQ):
            q, to = q_peer(i)
            copy(zs.at[s, ch, q], zr.at[s, ch, b_me], z_s.at[s, ch], z_r.at[s, ch], to, y).start()
        zr[s, ch, b_me] = zs[s, ch, b_me]

    def do_y(s):
        for ch in range(2):
            await_recv(zr.at[s, ch, pl.ds(0, NQ - 1)], z_r.at[s, ch])
        ys[s] = mm(sel[...].reshape(R, I), zr[s].reshape(I, W)).astype(BF).reshape(NL, Q, W)
        for i in range(1, NL):
            to = y_peer(i)
            copy(ys.at[s, to], yr.at[s, y], y_s.at[s], y_r.at[s], node, to).start()
        yr[s, y] = ys[s, y]

    def give_back(s, value):
        bs[s] = value.astype(BF).reshape(NL, Q, W)
        for i in range(1, NL):
            to = y_peer(i)
            copy(bs.at[s, to], br.at[s, y], b_s.at[s], b_r.at[s], node, to).start()
        br[s, y] = bs[s, y]

    def do_e(s):
        await_recv(yr.at[s, pl.ds(0, NL - 1)], y_r.at[s])
        rows = yr[s].reshape(R, W)
        u = s % NC
        cols = slice(u * W, (u + 1) * W)
        if s == 0:
            for w in weights:
                w.wait()
        if s < NC:
            a_g, a_u = mm(rows, wg[cols]), mm(rows, wu[cols])
            if u:
                a_g, a_u = a_g + ag[...], a_u + au[...]
            ag[...], au[...] = a_g, a_u
            if s == NC - 1:
                hid = (a_g * jax.nn.sigmoid(a_g) * a_u).astype(BF)
                for v in range(NC):
                    give_back(v, mm(hid, wd[:, v * W:(v + 1) * W]))
        else:
            back = mm_nt(rows, wd[:, cols])
            if u:
                back = back + bk[...]
            bk[...] = back
            if s == NS - 1:
                a_g, a_u = ag[...], au[...]
                sig = jax.nn.sigmoid(a_g)
                g_g = (back * a_u * sig * (1.0 + a_g * (1.0 - sig))).astype(BF)
                g_u = (back * a_g * sig).astype(BF)
                for v in range(NC):
                    rng = slice(v * W, (v + 1) * W)
                    give_back(NC + v, mm_nt(g_g, wg[rng]) + mm_nt(g_u, wu[rng]))

    b_seen = set()

    def do_m(s, ch):
        if s not in b_seen:
            b_seen.add(s)
            await_recv(br.at[s, pl.ds(0, NL - 1)], b_r.at[s])
        half = I // 2
        rzs[s, ch] = mm(selg[ch * half:(ch + 1) * half], br[s].reshape(R, W)).astype(BF).reshape(NQ, BL, W)
        for i in range(1, NQ):
            q, to = q_peer(i)
            copy(rzs.at[s, ch, q], rzr.at[s, ch, b_me], rz_s.at[s, ch], rz_r.at[s, ch], to, y).start()
        rzr[s, ch, b_me] = rzs[s, ch, b_me]

    def do_p(s, ch):
        await_recv(rzr.at[s, ch, pl.ds(0, NQ - 1)], rz_r.at[s, ch])
        part[s, ch * PC:(ch + 1) * PC] = mm(pickt[ch], rzr[s, ch].reshape(NQ * BL, W)).reshape(PC, TOK, W)

    def do_rs(s, h):
        for side, steps in ((0, rights), (1, lefts)):
            d, half = steps[c.NH - 1 - h]
            value = part[s, slot_of(c, d, side), half * c.H:(half + 1) * c.H]
            if h >= 2:
                await_recv(rsr.at[s, side, h - 2], rs_r.at[s, side, h - 2])
                value = value + rsr[s, side, h - 2].astype(F32)
            rss[s, side, h] = value.astype(BF)
            copy(rss.at[s, side, h], rsr.at[s, side, h], rs_s.at[s, side], rs_r.at[s, side, h],
                 x_peer(-1 if side == 0 else 1), y).start()

    def do_fin(s):
        out = mixed_ref if s < NC else igrad_ref
        cols = slice((s % NC) * W, (s % NC + 1) * W)
        values = [part[s, 0, v * c.H:(v + 1) * c.H] for v in range(2)]
        for side, steps in ((0, rights), (1, lefts)):
            for h in (c.NH - 2, c.NH - 1):
                await_recv(rsr.at[s, side, h], rs_r.at[s, side, h])
                half = steps[c.NH - 1 - h][1]
                values[half] = values[half] + rsr[s, side, h].astype(F32)
        for v in range(2):
            out[v * c.H:(v + 1) * c.H, cols] = values[v].astype(BF)

    def do_c1():
        cd = jnp.zeros((R, 1), F32)
        for u in range(NC):
            cd += jnp.sum(ys[NC + u].reshape(R, W).astype(F32) * br[u].reshape(R, W).astype(F32), axis=1, keepdims=True)
        spread = jnp.where(idiv(iota((R, LANES), 0), Q) == imod(iota((R, LANES), 1), NL), cd, 0.0).astype(BF)
        got = mm(selt[...], spread)
        mine = (idiv(iota((I, LANES), 1), NL) == imod(iota((I, LANES), 0), J)) & (iota((I, LANES), 1) < J * NL)
        got = jnp.where(mine, got, 0.0).astype(BF)
        n = NQ * NX
        fold = onehot(iota((n, I), 0) == slot_rows(iota((n, I), 1)))
        cm[...] = mm(fold, got).reshape(NQ, NX, LANES)
        c1r[b_me] = cm[b_me]
        for i in range(1, NQ):
            q, to = q_peer(i)
            copy(cm.at[q], c1r.at[b_me], s_small.at[2], r_small.at[2], to, y).start()

    def do_c2():
        await_recv(c1r.at[pl.ds(0, NQ - 1)], r_small.at[2])
        n = NX * NQ
        row, col = iota((n, n), 0), iota((n, n), 1)
        turn = onehot((imod(row, NQ) == idiv(col, NX)) & (idiv(row, NQ) == imod(col, NX)))
        c2s[...] = mm(turn, c1r[...].reshape(n, LANES).astype(BF)).reshape(NX, NQ, LANES)
        c2r[xx] = c2s[0]
        for p in range(1, NX):
            to = lax.rem(xx + (static_offset(p) + NX), NX)
            copy(c2s.at[p], c2r.at[xx], s_small.at[3], r_small.at[3], (zz * NX + to) * c.NK + k, y).start()

    def do_c3():
        await_recv(c2r.at[pl.ds(0, NX - 1)], r_small.at[3])
        rows = c2r[...].reshape(NX * NQ, LANES).astype(BF)
        codes = c.KG * NL
        tab = jnp.zeros((TOK, codes), F32)
        for s in range(c.KG):
            mine = mm(acat[s], rows) * pmask[s].astype(F32)
            spread = onehot((iota((codes, LANES), 0) == s * NL + imod(iota((codes, LANES), 1), NL)))
            tab += mm_nt(mine.astype(BF), spread)
        cho = cho_ref[...]
        code, entry = iota((TOK, codes), 1), iota((TOK, c.TOP), 1)
        out = jnp.zeros((TOK, c.TOP), F32)
        for n in range(c.TOP):
            value = jnp.sum(jnp.where(cho[:, n:n + 1] == code, tab, 0.0), axis=1, keepdims=True)
            out += jnp.where(entry == n, value, 0.0)
        coef_ref[...] = out.astype(BF)

    steps = {"ag": do_ag, "z": do_z, "y": do_y, "e": do_e, "m": do_m, "p": do_p, "rs": do_rs, "fin": do_fin,
             "meta1": do_meta1, "meta2": do_meta2, "pick": do_pick, "rank": do_rank,
             "c1": do_c1, "c2": do_c2, "c3": do_c3}
    for key in order:
        steps[key[0]](*key[1:])
        issued.add(key)

    for n, ref in enumerate((m1.at[pl.ds(0, NX - 1)], m2.at[pl.ds(0, NQ - 1)], c1r.at[pl.ds(0, NQ - 1)],
                             c2r.at[pl.ds(0, NX - 1)])):
        await_send(ref, s_small.at[n])
    for s in range(NS):
        await_send(xg.at[s, pl.ds(0, NX - 1)], ag_s.at[s])
        for ref, sem in ((zs, z_s), (rzs, rz_s)):
            for ch in range(2):
                await_send(ref.at[s, ch, pl.ds(0, NQ - 1)], sem.at[s, ch])
        await_send(ys.at[s, pl.ds(0, NL - 1)], y_s.at[s])
        await_send(bs.at[s, pl.ds(0, NL - 1)], b_s.at[s])
        for side in range(2):
            await_send(rss.at[s, side], rs_s.at[s, side])


def per_device(c, x, dy, fac, perm, cho, quota, wg, wu, wd):
    NX, NQ, NL, PC, J, Q, TOK, NS, W = c.NX, c.NQ, c.NL, c.PC, c.J, c.Q, c.TOK, c.NS, c.W
    order, _ = plan(c)
    dma = pltpu.SemaphoreType.DMA
    V = pltpu.VMEM
    C = NQ * c.BL
    scratch = [
        V((c.D, c.F), BF), V((c.D, c.F), BF), V((c.F, c.D), BF),
        V((NS, NX, TOK, W), BF),
        V((NS, 2, NQ, c.BL, W), BF), V((NS, 2, NQ, c.BL, W), BF),
        V((NS, NL, Q, W), BF), V((NS, NL, Q, W), BF),
        V((NS, NL, Q, W), BF), V((NS, NL, Q, W), BF),
        V((NS, 2, NQ, c.BL, W), BF), V((NS, 2, NQ, c.BL, W), BF),
        V((NS, NX, TOK, W), F32),
        V((NS, 2, c.NH, c.H, W), BF), V((NS, 2, c.NH, c.H, W), BF),
        V((2, C, PC * TOK), BF), V((2, PC * TOK, C), BF),
        V((NL, Q, c.I), BF), V((c.I, c.R), BF), V((c.I, c.R), BF),
        V((c.R, c.F), F32), V((c.R, c.F), F32), V((c.R, c.F), F32),
        V((NX, NQ, 128), F32), V((NX, NQ, 128), F32), V((NQ, NX, 128), F32), V((NQ, NX, 128), F32),
        V((NQ, NX, 128), F32), V((NQ, NX, 128), F32), V((NX, NQ, 128), F32), V((NX, NQ, 128), F32),
        V((c.KG, TOK, c.NN), BF), V((c.KG, TOK, 128), BF),
        dma((3,)), dma((4,)), dma((4,)),
        dma((NS,)), dma((NS, 2, c.NH)), dma((NS, 2)), dma((NS, 2)), dma((NS,)), dma((NS,)),
        dma((NS,)), dma((NS,)), dma((NS, 2)), dma((NS, 2)), dma((NS, 2)), dma((NS, 2, c.NH)),
    ]
    vm = pl.BlockSpec(memory_space=pltpu.VMEM)
    hbm = pl.BlockSpec(memory_space=pl.ANY)
    flops = 2 * c.R * c.D * c.F * 6
    return pl.pallas_call(
        functools.partial(kernel, c, order),
        out_shape=(jax.ShapeDtypeStruct((TOK, c.D), BF), jax.ShapeDtypeStruct((TOK, c.D), BF),
                   jax.ShapeDtypeStruct((TOK, c.TOP), BF)),
        in_specs=[vm] * 6 + [hbm] * 3,
        out_specs=(vm, vm, vm),
        scratch_shapes=scratch,
        compiler_params=pltpu.CompilerParams(collective_id=0, has_side_effects=True, vmem_limit_bytes=60 * 2**20),
        cost_estimate=pl.CostEstimate(flops=flops, bytes_accessed=4 * 2**20, transcendentals=c.R * c.F),
        name="expert_layer",
    )(x, dy, fac, perm, cho, quota.reshape(1, NL), wg, wu, wd)


def solution(mesh, **over):
    def step(x, dy, fac, perm, cho, quota, wg, wu, wd):
        c = config(mesh, x.shape[0], perm.shape[1], cho.shape[1], x.shape[1], wg.shape[2], **over)
        return per_device(c, x, dy, fac, perm, cho, quota, wg, wu, wd)

    rows = P(("node", "local"), None)
    cube = P(("node", "local"), None, None)
    return jax.shard_map(
        step,
        mesh=mesh,
        in_specs=(rows, rows, rows, rows, rows, P("node"), cube, cube, cube),
        out_specs=(rows, rows, rows),
        check_vma=False,
    )
```

time: 446 us -> 261 us (0.59)
  Pallas kernels: 0 us -> 254 us
  waiting for transfers between devices: 195 us -> 0 us
  local copies, waits for them, and re-layouts: 124 us -> 6.69 us
  starting transfers between devices: 68.3 us -> 0 us
  other arithmetic: 26.3 us -> 0 us
  blocking collectives: 17.6 us -> 0 us
  matrix products: 11.6 us -> 0 us
    pallas_call x0 -> x1, Pallas kernels: none -> 254 us  [per_device(): pl.pallas_call(functools.partial(kernel, c, order), out_shape=(jax.ShapeD...]
    all_to_all x11 -> x0, waiting for transfers between devices: 195 us -> none  [the longest x1 43.2 us: per_device(): lax.all_to_all(send_rows, 'node', split_axis=0, concat_axis=0, tiled=True)]
    all_to_all x11 -> x0, starting transfers between devices: 68.3 us -> none  [the longest x1 13.8 us: per_device(): lax.all_to_all(send_gates, 'node', split_axis=0, concat_axis=0, tiled=True)]
    scatter x3 -> x0, local copies, waits for them, and re-layouts: 45.7 us -> none  [the longest x1 23.1 us: specialist_choice_map(): token_provenance = jnp.full((discard_entry + 1,), capacity_slot_count, jn...]
    gather x17 -> x0, local copies, waits for them, and re-layouts: 36.6 us -> none  [the longest x5 9.37 us: token_grads(): return jnp.take_along_axis(picked, chosen_machine_specialist_tuples, axis=1)]
    reshape x22 -> x0, local copies, waits for them, and re-layouts: 24.4 us -> none  [the longest x2 4.99 us: token_sum(): picked = returned.reshape(-1, feature)[landing].astype(jnp.float32)]
    all_to_all x1 -> x0, blocking collectives: 17.6 us -> none  [per_device(): lax.all_to_all(weight_part.reshape(node_count, group_slots, local_count),...]
    scatter-add x2 -> x0, other arithmetic: 12.5 us -> none  [slot_sums(): jax.ops.segment_sum(terms.reshape(-1, feature), token_provenance.reshape(...]
  transfers between devices with their start and end apart: 11 -> 0, of which waited for: 10 -> 0; matrix products, arithmetic and copies ran while one was open for 31% -> 0% of each run, Pallas kernels for 0% -> 0%
where the time goes in v1:
time: 261 us
  Pallas kernels  254 us (97%)
  local copies, waits for them, and re-layouts  6.69 us (3%)
    pallas_call x1, Pallas kernels, per_device(): pl.pallas_call(functools.partial(kernel, c, order), out_shape=(jax.ShapeD...  254 us
    unnamed x11, local copies, waits for them, and re-layouts  5.28 us

profile of v1, /device:TPU:6, one launch (start us, length us, event | category | flops | bytes accessed | tf_op | source)
XLA Modules:
  0.0 260.9 jit_solution(14489966409604847328)
XLA Ops:
  0.6 0.0 copy-start.2
  0.6 1.4 copy.12.fac_ref
  2.0 0.0 copy-done.2
  2.0 0.0 copy-start.1
  2.0 0.7 copy.13.perm_ref
  2.8 0.0 copy-done.1
  2.8 0.7 copy.14.cho_ref
  3.5 253.5 %expert_layer.1 = (bf16[128,1024]{1,0:T(8,128)(2,1)}, bf16[128,1024]{1,0:T(8,128)(2,1)}, bf16[128,8]{1,0:T(8,128)(2,1)}) custom-call(bf16[128,1024]{1,0:T(8,128)(2,1)} %x_ref.1, bf16[128,1024]{1,0:T(8,128)(2,1)} %dy_ref.1, bf16[128,8]{1,0:T(8,128)(2,1)} %copy.12.fac_ref, s32[128,4]{1,0:T(8,128)} %copy.13.perm_ref, s32[128,8]{1,0:T(8,128)} %copy.14.cho_ref, ...), custom_call_target="tpu_custom_call" | custom-call | flops 2415919104 | bytes 4194304 | tf_op jit(solution)/shard_map/expert_layer/pallas_call | solution.py:531
  257.0 1.4 copy.15
  258.4 0.0 copy-start
  258.4 1.7 copy.18
  260.1 0.0 copy-done
  260.1 0.7 copy.19
Async XLA Ops:
  0.6 1.4 copy-start.2
  2.0 0.7 copy-start.1
  258.4 1.7 copy-start

commit v2 on v1

--- a/solution.py
+++ b/solution.py
@@ -17,9 +17,8 @@
 def config(mesh, tok, kg, top, feature, hidden, most=12, quota=48):
     c = SimpleNamespace()
     c.NN, c.NL = mesh.shape["node"], mesh.shape["local"]
-    c.NK, c.NX = (2, 8) if c.NN == 64 else (1, 4)
-    c.NZ = c.NN // (c.NK * c.NX)
-    c.NQ = c.NZ * c.NK
+    c.NX = 8 if c.NN == 64 else 4
+    c.NQ = c.NN // c.NX
     c.PC = c.NX // 2
     c.D2 = c.NX // 2
     c.NH = c.NX - 1
@@ -150,15 +149,14 @@
     NG, I, R, BL = c.NN, c.I, c.R, c.BL
     LANES = 128
     node, y = lax.axis_index("node"), lax.axis_index("local")
-    k, xx, zz = lax.rem(node, c.NK), lax.rem(lax.div(node, c.NK), NX), lax.div(node, c.NK * NX)
-    b_me = zz * c.NK + k
+    xx, b_me = lax.div(node, NQ), lax.rem(node, NQ)
 
     def x_peer(o):
-        return (zz * NX + lax.rem(xx + (o + NX), NX)) * c.NK + k
+        return lax.rem(xx + (o + NX), NX) * NQ + b_me
 
     def q_peer(i):
         q = lax.rem(b_me + i, NQ)
-        return q, (lax.div(q, c.NK) * NX + xx) * c.NK + lax.rem(q, c.NK)
+        return q, xx * NQ + q
 
     def y_peer(i):
         return lax.rem(y + i, NL)
@@ -236,9 +234,7 @@
         named = []
         for s in range(c.KG):
             g = perm[:, s:s + 1]
-            gx = imod(idiv(g, c.NK), NX)
-            gq = idiv(g, c.NK * NX) * c.NK + imod(g, c.NK)
-            named.append(jnp.where(gx * NQ + gq == groups, 1.0, 0.0))
+            named.append(jnp.where(g == groups, 1.0, 0.0))
         total = sum(named[1:], named[0]).astype(BF)
         lower = onehot(iota((TOK, TOK), 1) < iota((TOK, TOK), 0))
         place = mm(lower, total)
@@ -260,7 +256,7 @@
         m1[0] = meta[xx]
         for p in range(1, NX):
             to = lax.rem(xx + (NX - static_offset(p)), NX)
-            copy(meta.at[to], m1.at[p], s_small.at[0], r_small.at[0], (zz * NX + to) * c.NK + k, y).start()
+            copy(meta.at[to], m1.at[p], s_small.at[0], r_small.at[0], to * NQ + b_me, y).start()
 
     def do_meta2():
         await_recv(m1.at[pl.ds(0, NX - 1)], r_small.at[0])
@@ -312,7 +308,7 @@
 
         def number(r):
             b, p = idiv(r, NX), imod(r, NX)
-            return (idiv(b, c.NK) * NX + ((xx + offset_of(p) + NX) & (NX - 1))) * c.NK + imod(b, c.NK)
+            return ((xx + offset_of(p) + NX) & (NX - 1)) * NQ + b
 
         before = onehot(number(iota((n, n), 1)) < number(iota((n, n), 0)))
         rank = inside + mm(before, rows)
@@ -460,7 +456,7 @@
         c2r[xx] = c2s[0]
         for p in range(1, NX):
             to = lax.rem(xx + (static_offset(p) + NX), NX)
-            copy(c2s.at[p], c2r.at[xx], s_small.at[3], r_small.at[3], (zz * NX + to) * c.NK + k, y).start()
+            copy(c2s.at[p], c2r.at[xx], s_small.at[3], r_small.at[3], to * NQ + b_me, y).start()
 
     def do_c3():
         await_recv(c2r.at[pl.ds(0, NX - 1)], r_small.at[3])

time: 261 us -> 159 us (0.61)
  Pallas kernels: 254 us -> 150 us
    pallas_call x1, Pallas kernels: 254 us -> 150 us  [per_device(): pl.pallas_call(functools.partial(kernel, c, order), out_shape=(jax.ShapeD...]
where the time goes in v2:
time: 159 us; the launch traced here: 158 us
  Pallas kernels  150 us (94%)
  local copies, waits for them, and re-layouts  6.69 us (4%)
    pallas_call x1, Pallas kernels, per_device(): pl.pallas_call(functools.partial(kernel, c, order), out_shape=(jax.ShapeD...  150 us
    unnamed x11, local copies, waits for them, and re-layouts  5.28 us

profile of v2, /device:TPU:6, one launch (start us, length us, event | category | flops | bytes accessed | tf_op | source)
XLA Modules:
  0.0 157.5 jit_solution(338326714946861369)
XLA Ops:
  0.6 0.0 copy-start.2
  0.6 1.4 copy.12.fac_ref
  2.0 0.0 copy-done.2
  2.0 0.0 copy-start.1
  2.0 0.7 copy.13.perm_ref
  2.8 0.0 copy-done.1
  2.8 0.7 copy.14.cho_ref
  3.5 150.2 %expert_layer.1 = (bf16[128,1024]{1,0:T(8,128)(2,1)}, bf16[128,1024]{1,0:T(8,128)(2,1)}, bf16[128,8]{1,0:T(8,128)(2,1)}) custom-call(bf16[128,1024]{1,0:T(8,128)(2,1)} %x_ref.1, bf16[128,1024]{1,0:T(8,128)(2,1)} %dy_ref.1, bf16[128,8]{1,0:T(8,128)(2,1)} %copy.12.fac_ref, s32[128,4]{1,0:T(8,128)} %copy.13.perm_ref, s32[128,8]{1,0:T(8,128)} %copy.14.cho_ref, ...), custom_call_target="tpu_custom_call" | custom-call | flops 2415919104 | bytes 4194304 | tf_op jit(solution)/shard_map/expert_layer/pallas_call | solution.py:527
  153.7 1.4 copy.15
  155.1 0.0 copy-start
  155.1 1.7 %copy.18 = bf16[128,1024]{1,0:T(8,128)(2,1)} copy(bf16[128,1024]{1,0:T(8,128)(2,1)} %get-tuple-element.9) | data formatting | bytes 524288
  156.8 0.0 copy-done
  156.8 0.7 copy.19
Async XLA Ops:
  0.6 1.4 copy-start.2
  2.0 0.7 copy-start.1
  155.1 1.7 %copy-start = (bf16[128,1024]{1,0:T(8,128)(2,1)S(1)}, bf16[128,1024]{1,0:T(8,128)(2,1)}, u32[]{:S(2)}) copy-start(bf16[128,1024]{1,0:T(8,128)(2,1)} %get-tuple-element.10) | copy-start | bytes 786436

commit v3 on v2

--- a/solution.py
+++ b/solution.py
@@ -12,6 +12,47 @@
 MESH = pl.DeviceIdType.MESH
 BF = jnp.bfloat16
 F32 = jnp.float32
+
+
+INPUT_CUTS = ((2, 2, 2, 2), (2, 2, 2, 2))
+OUTPUT_CUTS = ((2, 2, 2, 2), (2, 2, 2, 2))
+
+ORDER = (
+    ("ag", 0, 0), ("ag", 1, 0), ("meta1",), ("ag", 0, 1), ("ag", 1, 1), ("ag", 2, 0), ("ag", 1, 2), ("ag", 0, 2),
+    ("ag", 1, 3), ("meta2",), ("ag", 0, 3), ("ag", 2, 2), ("pick",), ("ag", 1, 4), ("ag", 2, 1), ("ag", 0, 4), ("ag",
+    1, 5), ("z", 1, 0), ("ag", 1, 6), ("ag", 3, 0), ("z", 0, 0), ("ag", 0, 5), ("ag", 3, 1), ("ag", 0, 6), ("ag", 2,
+    3), ("ag", 2, 4), ("z", 1, 1), ("ag", 3, 2), ("rank",), ("ag", 3, 3), ("ag", 4, 0), ("z", 0, 1), ("ag", 2, 6),
+    ("ag", 2, 5), ("z", 2, 0), ("ag", 4, 1), ("ag", 3, 4), ("y", 1), ("ag", 4, 2), ("ag", 3, 5), ("z", 2, 1), ("z", 3,
+    0), ("ag", 4, 3), ("ag", 3, 6), ("y", 0), ("ag", 4, 4), ("ag", 5, 1), ("ag", 4, 5), ("ag", 7, 0), ("z", 3, 1),
+    ("ag", 4, 6), ("ag", 5, 0), ("z", 4, 0), ("ag", 6, 1), ("y", 2), ("ag", 6, 0), ("ag", 7, 1), ("z", 4, 1), ("ag",
+    5, 3), ("ag", 5, 2), ("ag", 7, 2), ("e", 0), ("ag", 6, 2), ("y", 3), ("ag", 6, 3), ("ag", 7, 3), ("ag", 5, 5),
+    ("e", 1), ("ag", 5, 4), ("z", 5, 0), ("ag", 7, 4), ("y", 4), ("ag", 7, 5), ("ag", 6, 4), ("z", 7, 0), ("e", 2),
+    ("ag", 5, 6), ("z", 6, 0), ("ag", 7, 6), ("ag", 6, 5), ("e", 3), ("b", 1), ("z", 5, 1), ("ag", 6, 6), ("b", 2),
+    ("z", 7, 1), ("b", 3), ("z", 6, 1), ("e", 4), ("m", 1, 1), ("m", 1, 0), ("y", 7), ("y", 5), ("m", 2, 1), ("p", 1,
+    1), ("rs", 1, 0), ("m", 3, 1), ("rs", 1, 1), ("m", 2, 0), ("rs", 1, 2), ("p", 2, 1), ("y", 6), ("rs", 2, 0), ("m",
+    3, 0), ("rs", 2, 1), ("p", 1, 0), ("b", 0), ("rs", 1, 3), ("p", 3, 1), ("rs", 3, 0), ("rs", 1, 4), ("rs", 3, 1),
+    ("rs", 2, 2), ("rs", 1, 5), ("p", 3, 0), ("p", 2, 0), ("rs", 2, 3), ("rs", 3, 2), ("rs", 1, 6), ("rs", 2, 4),
+    ("e", 5), ("rs", 3, 3), ("e", 6), ("e", 7), ("b", 4), ("rs", 3, 4), ("rs", 2, 5), ("rs", 2, 6), ("m", 0, 1), ("b",
+    7), ("rs", 3, 5), ("m", 0, 0), ("b", 5), ("rs", 3, 6), ("fin", 1), ("m", 4, 1), ("c1",), ("m", 4, 0), ("b", 6),
+    ("p", 0, 1), ("rs", 0, 0), ("rs", 0, 1), ("fin", 3), ("m", 7, 1), ("p", 4, 1), ("rs", 4, 0), ("rs", 0, 2), ("rs",
+    4, 1), ("p", 0, 0), ("rs", 0, 3), ("c2",), ("m", 5, 1), ("rs", 0, 4), ("m", 7, 0), ("p", 4, 0), ("rs", 4, 2),
+    ("p", 7, 1), ("rs", 7, 0), ("rs", 7, 1), ("rs", 4, 3), ("m", 6, 1), ("rs", 0, 5), ("m", 5, 0), ("p", 5, 1), ("rs",
+    5, 0), ("rs", 5, 1), ("rs", 7, 2), ("m", 6, 0), ("rs", 4, 4), ("rs", 0, 6), ("rs", 4, 5), ("p", 7, 0), ("rs", 5,
+    2), ("p", 6, 1), ("rs", 6, 0), ("rs", 7, 3), ("rs", 6, 1), ("rs", 7, 4), ("p", 5, 0), ("rs", 5, 3), ("rs", 6, 2),
+    ("rs", 5, 4), ("fin", 0), ("p", 6, 0), ("rs", 6, 3), ("c3",), ("rs", 4, 6), ("rs", 7, 5), ("rs", 6, 4), ("fin",
+    2), ("rs", 7, 6), ("rs", 5, 5), ("rs", 5, 6), ("rs", 6, 5), ("rs", 6, 6), ("fin", 4), ("fin", 7), ("fin", 5),
+    ("fin", 6),
+)
+
+
+def cut_columns(unit, cuts):
+    streams = []
+    for tensor, parts in enumerate(cuts):
+        first = 0
+        for part in parts:
+            streams.append((tensor, first, part * unit))
+            first += part * unit
+    return streams
 
 
 def config(mesh, tok, kg, top, feature, hidden, most=12, quota=48):
@@ -24,9 +65,10 @@
     c.NH = c.NX - 1
     c.TOK, c.KG, c.TOP, c.D, c.F = tok, kg, top, feature, hidden
     c.J, c.Q = most, quota
-    c.NC = 2
-    c.W = feature // c.NC
-    c.NS = 2 * c.NC
+    unit = feature // 8
+    c.inp = cut_columns(unit, INPUT_CUTS)
+    c.out = cut_columns(unit, OUTPUT_CUTS)
+    c.last = [max(s for s, (n, _, _) in enumerate(c.inp) if n == t) for t in range(2)]
     c.BL = c.PC * c.J
     c.I = 2 * c.NQ * c.BL
     c.R = c.NL * c.Q
@@ -48,46 +90,48 @@
     return 2 * d - 1 if (side == 0 or d == c.D2) else 2 * d
 
 
-def plan(c):
-    NS, NC, NH = c.NS, c.NC, c.NH
-    tx, tz, ty, lat = 1.4, 4.5, 9.0, 1.5
+def plan(c, prio=None, gate=(2, 4)):
+    NH = c.NH
+    prio = prio or {}
     tasks, links = {}, {}
+    hop, back, side, across = 2.0, 2.5, 3.5, 2.5
 
     def add(key, pri, cost, deps, sends=()):
-        tasks[key] = (pri, cost, deps, sends)
-
-    add(("meta1",), -9, 1.5, [], [(("M1",), "x", 0.2)])
-    add(("meta2",), -8, 0.5, [("M1",)], [(("M2",), "z", 0.2)])
-    add(("pick",), -7, 1.5, [("M1",)])
-    add(("rank",), -6, 2.0, [("M2",)])
-    for s in range(NS):
+        tasks[key] = (pri + prio.get(key, prio.get(key[0], 0)), cost, deps, sends)
+
+    add(("meta1",), -9, 0.6, [], [(("M1",), "z", 0.2, hop + 1)])
+    add(("meta2",), -8, 0.3, [("M1",)], [(("M2",), "x", 0.2, side)])
+    add(("pick",), -7, 0.6, [("meta2",)])
+    add(("rank",), -6, 1.6, [("M2",)])
+    near = 3 if c.D2 > 2 else NH - 1
+    for s, (t, _, width) in enumerate(c.inp):
+        f = width / c.D
         for h in range(NH):
-            deps = [("AG", s, h - 2)] if h >= 2 else ([("ag", s - 1, NH - 3)] if s else [])
-            add(("ag", s, h), s * 10 - 100, 0.1, deps, [(("AG", s, h), "x", tx)])
+            start = min(gate[0 if c.inp[s - 1][2] < c.D // 2 else 1], NH - 1)
+            deps = [("AG", s, h - 2)] if h >= 2 else ([("ag", s - 1, start)] if s else [])
+            add(("ag", s, h), s * 10 - 100, 0.15, deps, [(("AG", s, h), "z", 2.92 * f, hop)])
         for ch in range(2):
-            need = 3 if ch == 0 and c.D2 > 2 else NH - 1
-            deps = [("pick",)] + [("AG", s, g) for g in range(need + 1)]
-            add(("z", s, ch), s * 10 + ch, 0.8, deps, [(("Z", s, ch), "z", tz)])
-        add(("y", s), s * 10 + 3, 0.9, [("rank",), ("Z", s, 0), ("Z", s, 1)], [(("Y", s), "y", ty)])
-    for s in range(NS):
+            deps = [("pick",)] + [("AG", s, g) for g in range((near if ch == 0 else NH - 1) + 1)]
+            add(("z", s, ch), s * 10 + ch, 0.2 + 0.25 * f, deps, [(("Z", s, ch), "x", 9.2 * f, side)])
+        add(("y", s), s * 10 + 3, 0.2 + 0.6 * f, [("rank",), ("Z", s, 0), ("Z", s, 1)], [(("Y", s), "y", 18.4 * f, across)])
         deps = [("Y", s)] + ([("e", s - 1)] if s else [])
-        sends = []
-        if s == NC - 1:
-            sends = [(("B", u), "y", ty) for u in range(NC)]
-        if s == NS - 1:
-            sends = [(("B", u), "y", ty) for u in range(NC, NS)]
-        add(("e", s), s * 10 + 4, 2.0, deps, sends)
+        add(("e", s), s * 10 + 4, 0.1 + 0.6 * f + (0.5 if s in c.last else 0), deps)
+    for u, (t, _, width) in enumerate(c.out):
+        f = width / c.D
+        at = u * 10 + 4
+        add(("b", u), at + 0.5, 0.2 + 0.6 * f, [("e", c.last[t])], [(("B", u), "y", 18.4 * f, across)])
         for ch in (1, 0):
-            add(("m", s, ch), s * 10 + 5 - ch, 0.8, [("B", s)], [(("RZ", s, ch), "z", tz)])
-            add(("p", s, ch), s * 10 + 7 - ch, 0.8, [("RZ", s, ch)])
+            add(("m", u, ch), at + 1 - ch, 0.15 + 0.3 * f, [("B", u)], [(("RZ", u, ch), "x", 9.2 * f, side)])
+            add(("p", u, ch), at + 3 - ch, 0.1 + 0.4 * f, [("RZ", u, ch)])
         for h in range(NH):
-            deps = [("p", s, 1)] + ([("p", s, 0)] if h > (2 if c.D2 > 2 else 0) else [])
-            deps += [("RS", s, h - 2)] if h >= 2 else []
-            add(("rs", s, h), s * 10 - 90, 0.15, deps, [(("RS", s, h), "x", tx)])
-        add(("fin", s), s * 10 + 8, 0.3, [("p", s, 0), ("RS", s, NH - 1), ("RS", s, NH - 2)])
-    add(("c1",), 45, 1.0, [("m", u, 0) for u in range(NC)] + [("y", u) for u in range(NC, NS)], [(("C1",), "z", 0.2)])
-    add(("c2",), 46, 0.2, [("C1",)], [(("C2",), "x", 0.2)])
-    add(("c3",), 47, 0.5, [("C2",)])
+            deps = [("p", u, 1)] + ([("p", u, 0)] if h > (2 if c.D2 > 2 else 0) else [])
+            deps += [("RS", u, h - 2)] if h >= 2 else []
+            add(("rs", u, h), u * 10 - 90, 0.15, deps, [(("RS", u, h), "z", 2.92 * f, back)])
+        add(("fin", u), at + 4, 0.2, [("p", u, 0), ("RS", u, NH - 1), ("RS", u, NH - 2)])
+    mixes = [u for u, (t, _, _) in enumerate(c.out) if t == 0]
+    add(("c1",), 25, 0.6, [("m", u, 0) for u in mixes] + [("y", s) for s, (t, _, _) in enumerate(c.inp) if t], [(("C1",), "x", 0.2, side)])
+    add(("c2",), 26, 0.2, [("C1",)], [(("C2",), "z", 0.2, hop + 1)])
+    add(("c3",), 27, 0.4, [("C2",)])
 
     done, now, order = {}, 0.0, []
     left = dict(tasks)
@@ -104,7 +148,7 @@
         pri, cost, deps, sends = left.pop(key)
         now = best[0][0] + cost
         done[key] = now
-        for event, link, length in sends:
+        for event, link, length, lat in sends:
             start = max(now, links.get(link, 0.0))
             links[link] = start + length
             done[event] = start + length + lat
@@ -141,12 +185,19 @@
 
 
 def kernel(c, order, x_ref, dy_ref, fac_ref, perm_ref, cho_ref, quota_ref, wg_hbm, wu_hbm, wd_hbm,
-           mixed_ref, igrad_ref, coef_ref,
-           wg, wu, wd, xg, zs, zr, ys, yr, bs, br, rzs, rzr, part, rss, rsr,
-           pick, pickt, sel, selt, selg, ag, au, bk, meta, m1, m2s, m2, cm, c1r, c2s, c2r, acat, pmask,
-           w_sem, s_small, r_small, ag_s, ag_r, z_s, z_r, y_s, y_r, b_s, b_r, rz_s, rz_r, rs_s, rs_r):
-    NX, NQ, NL, PC, J, Q, TOK, NS, NC, W = c.NX, c.NQ, c.NL, c.PC, c.J, c.Q, c.TOK, c.NS, c.NC, c.W
+           mixed_ref, igrad_ref, coef_ref, *scratch):
+    NX, NQ, NL, PC, J, Q, TOK = c.NX, c.NQ, c.NL, c.PC, c.J, c.Q, c.TOK
     NG, I, R, BL = c.NN, c.I, c.R, c.BL
+    NI, NO = len(c.inp), len(c.out)
+    refs = list(scratch)
+
+    def take(n):
+        return [refs.pop(0) for _ in range(n)]
+
+    xg, zs, zr, ys, yr = [take(NI) for _ in range(5)]
+    bs, br, rzs, rzr, part, rss, rsr = [take(NO) for _ in range(7)]
+    (wg, wu, wd, pick, pickt, sel, selt, selg, ag, au, bk, hid, g_g, g_u, meta, m1, m2s, m2, cm, c1r, c2s, c2r, acat,
+     pmask, cols_ref, w_sem, s_small, r_small, ag_s, ag_r, z_s, z_r, y_s, y_r, b_s, b_r, rz_s, rz_r, rs_s, rs_r) = refs
     LANES = 128
     node, y = lax.axis_index("node"), lax.axis_index("local")
     xx, b_me = lax.div(node, NQ), lax.rem(node, NQ)
@@ -183,9 +234,8 @@
                for n, (h, v) in enumerate(((wg_hbm, wg), (wu_hbm, wu), (wd_hbm, wd)))]
     for w in weights:
         w.start()
-    for s in range(NS):
-        src = x_ref if s < NC else dy_ref
-        xg[s, 0] = src[:, (s % NC) * W:(s % NC + 1) * W]
+    for s, (t, first, width) in enumerate(c.inp):
+        xg[s][0] = (dy_ref if t else x_ref)[:, first:first + width]
     pl.semaphore_wait(barrier, (NX - 1) + (NQ - 1) + (NL - 1))
 
     rights, lefts = ring_steps(c)
@@ -202,28 +252,32 @@
         for side, steps in ((0, rights), (1, lefts)):
             if h >= 2 and (s, h - 2) not in waited:
                 d0, h0 = steps[h - 2]
-                await_recv(xg.at[s, slot_of(c, d0, side), pl.ds(h0 * c.H, c.H)], ag_r.at[s, side, h - 2])
+                await_recv(xg[s].at[slot_of(c, d0, side), pl.ds(h0 * c.H, c.H)], ag_r.at[s, side, h - 2])
             d, half = steps[h]
             rows = pl.ds(half * c.H, c.H)
-            copy(xg.at[s, slot_of(c, d - 1, side), rows], xg.at[s, slot_of(c, d, side), rows],
+            copy(xg[s].at[slot_of(c, d - 1, side), rows], xg[s].at[slot_of(c, d, side), rows],
                  ag_s.at[s], ag_r.at[s, side, h], x_peer(1 if side == 0 else -1), y).start()
 
-    ag_seen = {s: 0 for s in range(NS)}
+    ag_seen = {s: 0 for s in range(NI)}
 
     def ag_upto(s, h):
         for g in range(ag_seen[s], h + 1):
             if g + 2 >= c.NH or (("ag", s, g + 2) not in issued):
                 for side, steps in ((0, rights), (1, lefts)):
                     d0, h0 = steps[g]
-                    await_recv(xg.at[s, slot_of(c, d0, side), pl.ds(h0 * c.H, c.H)], ag_r.at[s, side, g])
+                    await_recv(xg[s].at[slot_of(c, d0, side), pl.ds(h0 * c.H, c.H)], ag_r.at[s, side, g])
                 waited.add((s, g))
         ag_seen[s] = max(ag_seen[s], h + 1)
 
     issued, waited = set(), set()
 
     def do_meta1():
-        perm, cho = perm_ref[...], cho_ref[...]
-        fac = fac_ref[...].astype(F32)
+        table = jnp.concatenate([v[...].astype(F32) for v in (cho_ref, fac_ref, perm_ref)], axis=0).astype(BF)
+        eye = onehot(iota((TOK, TOK), 0) == iota((TOK, TOK), 1))
+        turned = mm_nt(eye, table)
+        cols_ref[...] = turned
+        cho, perm = turned.astype(jnp.int32), turned[:, 2 * c.TOP:].astype(jnp.int32)
+        fac = turned[:, c.TOP:2 * c.TOP]
         lane = iota((TOK, LANES), 1)
         code = iota((TOK, c.KG * NL), 1)
         table = jnp.zeros((TOK, c.KG * NL), F32)
@@ -337,104 +391,115 @@
 
     def do_z(s, ch):
         ag_upto(s, 3 if ch == 0 and c.D2 > 2 else c.NH - 1)
-        rows = xg[s, ch * PC:(ch + 1) * PC].reshape(PC * TOK, W)
-        zs[s, ch] = mm(pick[ch], rows).astype(BF).reshape(NQ, BL, W)
+        width = c.inp[s][2]
+        rows = xg[s][ch * PC:(ch + 1) * PC].reshape(PC * TOK, width)
+        zs[s][ch] = mm(pick[ch], rows).astype(BF).reshape(NQ, BL, width)
         for i in range(1, NQ):
             q, to = q_peer(i)
-            copy(zs.at[s, ch, q], zr.at[s, ch, b_me], z_s.at[s, ch], z_r.at[s, ch], to, y).start()
-        zr[s, ch, b_me] = zs[s, ch, b_me]
+            copy(zs[s].at[ch, q], zr[s].at[ch, b_me], z_s.at[s, ch], z_r.at[s, ch], to, y).start()
+        zr[s][ch, b_me] = zs[s][ch, b_me]
 
     def do_y(s):
+        width = c.inp[s][2]
         for ch in range(2):
-            await_recv(zr.at[s, ch, pl.ds(0, NQ - 1)], z_r.at[s, ch])
-        ys[s] = mm(sel[...].reshape(R, I), zr[s].reshape(I, W)).astype(BF).reshape(NL, Q, W)
+            await_recv(zr[s].at[ch, pl.ds(0, NQ - 1)], z_r.at[s, ch])
+        ys[s][...] = mm(sel[...].reshape(R, I), zr[s][...].reshape(I, width)).astype(BF).reshape(NL, Q, width)
         for i in range(1, NL):
             to = y_peer(i)
-            copy(ys.at[s, to], yr.at[s, y], y_s.at[s], y_r.at[s], node, to).start()
-        yr[s, y] = ys[s, y]
-
-    def give_back(s, value):
-        bs[s] = value.astype(BF).reshape(NL, Q, W)
-        for i in range(1, NL):
-            to = y_peer(i)
-            copy(bs.at[s, to], br.at[s, y], b_s.at[s], b_r.at[s], node, to).start()
-        br[s, y] = bs[s, y]
+            copy(ys[s].at[to], yr[s].at[y], y_s.at[s], y_r.at[s], node, to).start()
+        yr[s][y] = ys[s][y]
 
     def do_e(s):
-        await_recv(yr.at[s, pl.ds(0, NL - 1)], y_r.at[s])
-        rows = yr[s].reshape(R, W)
-        u = s % NC
-        cols = slice(u * W, (u + 1) * W)
+        await_recv(yr[s].at[pl.ds(0, NL - 1)], y_r.at[s])
+        t, first, width = c.inp[s]
+        rows = yr[s][...].reshape(R, width)
+        cols = slice(first, first + width)
         if s == 0:
             for w in weights:
                 w.wait()
-        if s < NC:
+        if t == 0:
             a_g, a_u = mm(rows, wg[cols]), mm(rows, wu[cols])
-            if u:
+            if first:
                 a_g, a_u = a_g + ag[...], a_u + au[...]
             ag[...], au[...] = a_g, a_u
-            if s == NC - 1:
-                hid = (a_g * jax.nn.sigmoid(a_g) * a_u).astype(BF)
-                for v in range(NC):
-                    give_back(v, mm(hid, wd[:, v * W:(v + 1) * W]))
+            if s == c.last[0]:
+                hid[...] = (a_g * jax.nn.sigmoid(a_g) * a_u).astype(BF)
         else:
             back = mm_nt(rows, wd[:, cols])
-            if u:
+            if first:
                 back = back + bk[...]
             bk[...] = back
-            if s == NS - 1:
+            if s == c.last[1]:
                 a_g, a_u = ag[...], au[...]
                 sig = jax.nn.sigmoid(a_g)
-                g_g = (back * a_u * sig * (1.0 + a_g * (1.0 - sig))).astype(BF)
-                g_u = (back * a_g * sig).astype(BF)
-                for v in range(NC):
-                    rng = slice(v * W, (v + 1) * W)
-                    give_back(NC + v, mm_nt(g_g, wg[rng]) + mm_nt(g_u, wu[rng]))
+                g_g[...] = (back * a_u * sig * (1.0 + a_g * (1.0 - sig))).astype(BF)
+                g_u[...] = (back * a_g * sig).astype(BF)
+
+    def do_b(u):
+        t, first, width = c.out[u]
+        cols = slice(first, first + width)
+        if t == 0:
+            value = mm(hid[...], wd[:, cols])
+        else:
+            value = mm_nt(g_g[...], wg[cols]) + mm_nt(g_u[...], wu[cols])
+        bs[u][...] = value.astype(BF).reshape(NL, Q, width)
+        for i in range(1, NL):
+            to = y_peer(i)
+            copy(bs[u].at[to], br[u].at[y], b_s.at[u], b_r.at[u], node, to).start()
+        br[u][y] = bs[u][y]
 
     b_seen = set()
 
-    def do_m(s, ch):
-        if s not in b_seen:
-            b_seen.add(s)
-            await_recv(br.at[s, pl.ds(0, NL - 1)], b_r.at[s])
+    def do_m(u, ch):
+        width = c.out[u][2]
+        if u not in b_seen:
+            b_seen.add(u)
+            await_recv(br[u].at[pl.ds(0, NL - 1)], b_r.at[u])
         half = I // 2
-        rzs[s, ch] = mm(selg[ch * half:(ch + 1) * half], br[s].reshape(R, W)).astype(BF).reshape(NQ, BL, W)
+        rzs[u][ch] = mm(selg[ch * half:(ch + 1) * half], br[u][...].reshape(R, width)).astype(BF).reshape(NQ, BL, width)
         for i in range(1, NQ):
             q, to = q_peer(i)
-            copy(rzs.at[s, ch, q], rzr.at[s, ch, b_me], rz_s.at[s, ch], rz_r.at[s, ch], to, y).start()
-        rzr[s, ch, b_me] = rzs[s, ch, b_me]
-
-    def do_p(s, ch):
-        await_recv(rzr.at[s, ch, pl.ds(0, NQ - 1)], rz_r.at[s, ch])
-        part[s, ch * PC:(ch + 1) * PC] = mm(pickt[ch], rzr[s, ch].reshape(NQ * BL, W)).reshape(PC, TOK, W)
-
-    def do_rs(s, h):
+            copy(rzs[u].at[ch, q], rzr[u].at[ch, b_me], rz_s.at[u, ch], rz_r.at[u, ch], to, y).start()
+        rzr[u][ch, b_me] = rzs[u][ch, b_me]
+
+    def do_p(u, ch):
+        width = c.out[u][2]
+        await_recv(rzr[u].at[ch, pl.ds(0, NQ - 1)], rz_r.at[u, ch])
+        sums = mm(pickt[ch], rzr[u][ch].reshape(NQ * BL, width))
+        part[u][ch * PC:(ch + 1) * PC] = sums.reshape(PC, TOK, width)
+
+    def do_rs(u, h):
         for side, steps in ((0, rights), (1, lefts)):
             d, half = steps[c.NH - 1 - h]
-            value = part[s, slot_of(c, d, side), half * c.H:(half + 1) * c.H]
+            value = part[u][slot_of(c, d, side), half * c.H:(half + 1) * c.H]
             if h >= 2:
-                await_recv(rsr.at[s, side, h - 2], rs_r.at[s, side, h - 2])
-                value = value + rsr[s, side, h - 2].astype(F32)
-            rss[s, side, h] = value.astype(BF)
-            copy(rss.at[s, side, h], rsr.at[s, side, h], rs_s.at[s, side], rs_r.at[s, side, h],
+                await_recv(rsr[u].at[side, h - 2], rs_r.at[u, side, h - 2])
+                value = value + rsr[u][side, h - 2].astype(F32)
+            rss[u][side, h] = value.astype(BF)
+            copy(rss[u].at[side, h], rsr[u].at[side, h], rs_s.at[u, side], rs_r.at[u, side, h],
                  x_peer(-1 if side == 0 else 1), y).start()
 
-    def do_fin(s):
-        out = mixed_ref if s < NC else igrad_ref
-        cols = slice((s % NC) * W, (s % NC + 1) * W)
-        values = [part[s, 0, v * c.H:(v + 1) * c.H] for v in range(2)]
+    def do_fin(u):
+        t, first, width = c.out[u]
+        out = igrad_ref if t else mixed_ref
+        values = [part[u][0, v * c.H:(v + 1) * c.H] for v in range(2)]
         for side, steps in ((0, rights), (1, lefts)):
             for h in (c.NH - 2, c.NH - 1):
-                await_recv(rsr.at[s, side, h], rs_r.at[s, side, h])
+                await_recv(rsr[u].at[side, h], rs_r.at[u, side, h])
                 half = steps[c.NH - 1 - h][1]
-                values[half] = values[half] + rsr[s, side, h].astype(F32)
+                values[half] = values[half] + rsr[u][side, h].astype(F32)
         for v in range(2):
-            out[v * c.H:(v + 1) * c.H, cols] = values[v].astype(BF)
+            out[v * c.H:(v + 1) * c.H, first:first + width] = values[v].astype(BF)
 
     def do_c1():
         cd = jnp.zeros((R, 1), F32)
-        for u in range(NC):
-            cd += jnp.sum(ys[NC + u].reshape(R, W).astype(F32) * br[u].reshape(R, W).astype(F32), axis=1, keepdims=True)
+        for s, (t, first, width) in enumerate(c.inp):
+            for u, (v, begin, size) in enumerate(c.out):
+                low, high = max(first, begin), min(first + width, begin + size)
+                if t == 1 and v == 0 and low < high:
+                    up = ys[s][:, :, low - first:high - first].reshape(R, high - low).astype(F32)
+                    got = br[u][:, :, low - begin:high - begin].reshape(R, high - low).astype(F32)
+                    cd += jnp.sum(up * got, axis=1, keepdims=True)
         spread = jnp.where(idiv(iota((R, LANES), 0), Q) == imod(iota((R, LANES), 1), NL), cd, 0.0).astype(BF)
         got = mm(selt[...], spread)
         mine = (idiv(iota((I, LANES), 1), NL) == imod(iota((I, LANES), 0), J)) & (iota((I, LANES), 1) < J * NL)
@@ -467,15 +532,16 @@
             mine = mm(acat[s], rows) * pmask[s].astype(F32)
             spread = onehot((iota((codes, LANES), 0) == s * NL + imod(iota((codes, LANES), 1), NL)))
             tab += mm_nt(mine.astype(BF), spread)
-        cho = cho_ref[...]
+        cho = cols_ref[...].astype(jnp.int32)
         code, entry = iota((TOK, codes), 1), iota((TOK, c.TOP), 1)
         out = jnp.zeros((TOK, c.TOP), F32)
         for n in range(c.TOP):
             value = jnp.sum(jnp.where(cho[:, n:n + 1] == code, tab, 0.0), axis=1, keepdims=True)
             out += jnp.where(entry == n, value, 0.0)
-        coef_ref[...] = out.astype(BF)
-
-    steps = {"ag": do_ag, "z": do_z, "y": do_y, "e": do_e, "m": do_m, "p": do_p, "rs": do_rs, "fin": do_fin,
+        eye = onehot(iota((c.TOP, c.TOP), 0) == iota((c.TOP, c.TOP), 1))
+        coef_ref[...] = mm_nt(eye, out.astype(BF)).astype(BF)
+
+    steps = {"ag": do_ag, "z": do_z, "y": do_y, "e": do_e, "b": do_b, "m": do_m, "p": do_p, "rs": do_rs, "fin": do_fin,
              "meta1": do_meta1, "meta2": do_meta2, "pick": do_pick, "rank": do_rank,
              "c1": do_c1, "c2": do_c2, "c3": do_c3}
     for key in order:
@@ -485,56 +551,60 @@
     for n, ref in enumerate((m1.at[pl.ds(0, NX - 1)], m2.at[pl.ds(0, NQ - 1)], c1r.at[pl.ds(0, NQ - 1)],
                              c2r.at[pl.ds(0, NX - 1)])):
         await_send(ref, s_small.at[n])
-    for s in range(NS):
-        await_send(xg.at[s, pl.ds(0, NX - 1)], ag_s.at[s])
-        for ref, sem in ((zs, z_s), (rzs, rz_s)):
-            for ch in range(2):
-                await_send(ref.at[s, ch, pl.ds(0, NQ - 1)], sem.at[s, ch])
-        await_send(ys.at[s, pl.ds(0, NL - 1)], y_s.at[s])
-        await_send(bs.at[s, pl.ds(0, NL - 1)], b_s.at[s])
+    for s in range(NI):
+        await_send(xg[s].at[pl.ds(0, NX - 1)], ag_s.at[s])
+        for ch in range(2):
+            await_send(zs[s].at[ch, pl.ds(0, NQ - 1)], z_s.at[s, ch])
+        await_send(ys[s].at[pl.ds(0, NL - 1)], y_s.at[s])
+    for u in range(NO):
+        for ch in range(2):
+            await_send(rzs[u].at[ch, pl.ds(0, NQ - 1)], rz_s.at[u, ch])
+        await_send(bs[u].at[pl.ds(0, NL - 1)], b_s.at[u])
         for side in range(2):
-            await_send(rss.at[s, side], rs_s.at[s, side])
+            await_send(rss[u].at[side], rs_s.at[u, side])
 
 
 def per_device(c, x, dy, fac, perm, cho, quota, wg, wu, wd):
-    NX, NQ, NL, PC, J, Q, TOK, NS, W = c.NX, c.NQ, c.NL, c.PC, c.J, c.Q, c.TOK, c.NS, c.W
-    order, _ = plan(c)
+    NX, NQ, NL, PC, Q, TOK = c.NX, c.NQ, c.NL, c.PC, c.Q, c.TOK
+    NI, NO = len(c.inp), len(c.out)
+    order = ORDER if c.NX == 8 else plan(c)[0]
     dma = pltpu.SemaphoreType.DMA
     V = pltpu.VMEM
     C = NQ * c.BL
-    scratch = [
+    scratch = []
+    for lead, kind, streams in (
+        ((NX, TOK), BF, c.inp), ((2, NQ, c.BL), BF, c.inp), ((2, NQ, c.BL), BF, c.inp), ((NL, Q), BF, c.inp), ((NL, Q), BF, c.inp),
+        ((NL, Q), BF, c.out), ((NL, Q), BF, c.out), ((2, NQ, c.BL), BF, c.out), ((2, NQ, c.BL), BF, c.out),
+        ((NX, TOK), F32, c.out), ((2, c.NH, c.H), BF, c.out), ((2, c.NH, c.H), BF, c.out),
+    ):
+        scratch += [V(lead + (width,), kind) for _, _, width in streams]
+    scratch += [
         V((c.D, c.F), BF), V((c.D, c.F), BF), V((c.F, c.D), BF),
-        V((NS, NX, TOK, W), BF),
-        V((NS, 2, NQ, c.BL, W), BF), V((NS, 2, NQ, c.BL, W), BF),
-        V((NS, NL, Q, W), BF), V((NS, NL, Q, W), BF),
-        V((NS, NL, Q, W), BF), V((NS, NL, Q, W), BF),
-        V((NS, 2, NQ, c.BL, W), BF), V((NS, 2, NQ, c.BL, W), BF),
-        V((NS, NX, TOK, W), F32),
-        V((NS, 2, c.NH, c.H, W), BF), V((NS, 2, c.NH, c.H, W), BF),
         V((2, C, PC * TOK), BF), V((2, PC * TOK, C), BF),
         V((NL, Q, c.I), BF), V((c.I, c.R), BF), V((c.I, c.R), BF),
-        V((c.R, c.F), F32), V((c.R, c.F), F32), V((c.R, c.F), F32),
+        V((c.R, c.F), F32), V((c.R, c.F), F32), V((c.R, c.F), F32), V((c.R, c.F), BF), V((c.R, c.F), BF), V((c.R, c.F), BF),
         V((NX, NQ, 128), F32), V((NX, NQ, 128), F32), V((NQ, NX, 128), F32), V((NQ, NX, 128), F32),
         V((NQ, NX, 128), F32), V((NQ, NX, 128), F32), V((NX, NQ, 128), F32), V((NX, NQ, 128), F32),
-        V((c.KG, TOK, c.NN), BF), V((c.KG, TOK, 128), BF),
+        V((c.KG, TOK, c.NN), BF), V((c.KG, TOK, 128), BF), V((TOK, 2 * c.TOP + c.KG), F32),
         dma((3,)), dma((4,)), dma((4,)),
-        dma((NS,)), dma((NS, 2, c.NH)), dma((NS, 2)), dma((NS, 2)), dma((NS,)), dma((NS,)),
-        dma((NS,)), dma((NS,)), dma((NS, 2)), dma((NS, 2)), dma((NS, 2)), dma((NS, 2, c.NH)),
+        dma((NI,)), dma((NI, 2, c.NH)), dma((NI, 2)), dma((NI, 2)), dma((NI,)), dma((NI,)),
+        dma((NO,)), dma((NO,)), dma((NO, 2)), dma((NO, 2)), dma((NO, 2)), dma((NO, 2, c.NH)),
     ]
     vm = pl.BlockSpec(memory_space=pltpu.VMEM)
     hbm = pl.BlockSpec(memory_space=pl.ANY)
     flops = 2 * c.R * c.D * c.F * 6
-    return pl.pallas_call(
+    mixed, grads, coef = pl.pallas_call(
         functools.partial(kernel, c, order),
         out_shape=(jax.ShapeDtypeStruct((TOK, c.D), BF), jax.ShapeDtypeStruct((TOK, c.D), BF),
-                   jax.ShapeDtypeStruct((TOK, c.TOP), BF)),
+                   jax.ShapeDtypeStruct((c.TOP, TOK), BF)),
         in_specs=[vm] * 6 + [hbm] * 3,
         out_specs=(vm, vm, vm),
         scratch_shapes=scratch,
         compiler_params=pltpu.CompilerParams(collective_id=0, has_side_effects=True, vmem_limit_bytes=60 * 2**20),
         cost_estimate=pl.CostEstimate(flops=flops, bytes_accessed=4 * 2**20, transcendentals=c.R * c.F),
         name="expert_layer",
-    )(x, dy, fac, perm, cho, quota.reshape(1, NL), wg, wu, wd)
+    )(x, dy, fac.T, perm.T, cho.T, quota.reshape(1, NL), wg, wu, wd)
+    return mixed, grads, coef.T
 
 
 def solution(mesh, **over):

time: 159 us -> 139 us (0.87)
  Pallas kernels: 150 us -> 135 us
  local copies, waits for them, and re-layouts: 6.69 us -> 3 us
    pallas_call x1, Pallas kernels: 150 us -> 135 us  [per_device(): pl.pallas_call(functools.partial(kernel, c, order), out_shape=(jax.ShapeD...]
    unnamed x11 -> x7, local copies, waits for them, and re-layouts: 5.28 us -> 3 us
where the time goes in v3:
time: 139 us
  Pallas kernels  135 us (97%)
  local copies, waits for them, and re-layouts  3 us (2%)
    pallas_call x1, Pallas kernels, per_device(): pl.pallas_call(functools.partial(kernel, c, order), out_shape=(jax.ShapeD...  135 us
    unnamed x7, local copies, waits for them, and re-layouts  3 us

profile of v3, /device:TPU:6, one launch (start us, length us, event | category | flops | bytes accessed | tf_op | source)
XLA Modules:
  0.0 138.6 jit_solution(3635475182852595164)
XLA Ops:
  0.6 134.9 %expert_layer.1 = (bf16[128,1024]{1,0:T(8,128)(2,1)}, bf16[128,1024]{1,0:T(8,128)(2,1)}, bf16[8,128]{1,0:T(8,128)(2,1)}) custom-call(bf16[128,1024]{1,0:T(8,128)(2,1)} %x_ref.1, bf16[128,1024]{1,0:T(8,128)(2,1)} %dy_ref.1, bf16[8,128]{1,0:T(8,128)(2,1)} %bitcast.7, s32[4,128]{1,0:T(4,128)} %bitcast.8, s32[8,128]{1,0:T(8,128)} %bitcast.6, s32[1,8]{1,0:T(1,128)} %bitcast.9, ...), custom_call_target="tpu_custom_call" | custom-call | flops 2415919104 | bytes 4194304 | tf_op jit(solution)/shard_map/expert_layer/pallas_call | solution.py:596
  135.6 0.0 copy-start
  135.6 1.7 %copy.15 = bf16[128,1024]{1,0:T(8,128)(2,1)} copy(bf16[128,1024]{1,0:T(8,128)(2,1)} %get-tuple-element.12) | data formatting | bytes 524288
  137.3 0.0 copy-done
  137.3 0.0 copy-start.1
  137.3 0.7 copy.16
  138.0 0.0 copy-done.1
  138.0 0.6 copy.17
Async XLA Ops:
  135.6 1.7 %copy-start = (bf16[128,1024]{1,0:T(8,128)(2,1)S(1)}, bf16[128,1024]{1,0:T(8,128)(2,1)}, u32[]{:S(2)}) copy-start(bf16[128,1024]{1,0:T(8,128)(2,1)} %get-tuple-element.13) | copy-start | bytes 786436
  137.3 0.7 copy-start.1

commit v4 on v3

--- a/solution.py
+++ b/solution.py
@@ -14,34 +14,31 @@
 F32 = jnp.float32
 
 
-INPUT_CUTS = ((2, 2, 2, 2), (2, 2, 2, 2))
-OUTPUT_CUTS = ((2, 2, 2, 2), (2, 2, 2, 2))
+INPUT_CUTS = ((2, 2, 2, 2), (2, 2, 4))
+OUTPUT_CUTS = ((2, 2, 4), (2, 2, 2, 2))
 
 ORDER = (
-    ("ag", 0, 0), ("ag", 1, 0), ("meta1",), ("ag", 0, 1), ("ag", 1, 1), ("ag", 2, 0), ("ag", 1, 2), ("ag", 0, 2),
-    ("ag", 1, 3), ("meta2",), ("ag", 0, 3), ("ag", 2, 2), ("pick",), ("ag", 1, 4), ("ag", 2, 1), ("ag", 0, 4), ("ag",
-    1, 5), ("z", 1, 0), ("ag", 1, 6), ("ag", 3, 0), ("z", 0, 0), ("ag", 0, 5), ("ag", 3, 1), ("ag", 0, 6), ("ag", 2,
-    3), ("ag", 2, 4), ("z", 1, 1), ("ag", 3, 2), ("rank",), ("ag", 3, 3), ("ag", 4, 0), ("z", 0, 1), ("ag", 2, 6),
-    ("ag", 2, 5), ("z", 2, 0), ("ag", 4, 1), ("ag", 3, 4), ("y", 1), ("ag", 4, 2), ("ag", 3, 5), ("z", 2, 1), ("z", 3,
-    0), ("ag", 4, 3), ("ag", 3, 6), ("y", 0), ("ag", 4, 4), ("ag", 5, 1), ("ag", 4, 5), ("ag", 7, 0), ("z", 3, 1),
-    ("ag", 4, 6), ("ag", 5, 0), ("z", 4, 0), ("ag", 6, 1), ("y", 2), ("ag", 6, 0), ("ag", 7, 1), ("z", 4, 1), ("ag",
-    5, 3), ("ag", 5, 2), ("ag", 7, 2), ("e", 0), ("ag", 6, 2), ("y", 3), ("ag", 6, 3), ("ag", 7, 3), ("ag", 5, 5),
-    ("e", 1), ("ag", 5, 4), ("z", 5, 0), ("ag", 7, 4), ("y", 4), ("ag", 7, 5), ("ag", 6, 4), ("z", 7, 0), ("e", 2),
-    ("ag", 5, 6), ("z", 6, 0), ("ag", 7, 6), ("ag", 6, 5), ("e", 3), ("b", 1), ("z", 5, 1), ("ag", 6, 6), ("b", 2),
-    ("z", 7, 1), ("b", 3), ("z", 6, 1), ("e", 4), ("m", 1, 1), ("m", 1, 0), ("y", 7), ("y", 5), ("m", 2, 1), ("p", 1,
-    1), ("rs", 1, 0), ("m", 3, 1), ("rs", 1, 1), ("m", 2, 0), ("rs", 1, 2), ("p", 2, 1), ("y", 6), ("rs", 2, 0), ("m",
-    3, 0), ("rs", 2, 1), ("p", 1, 0), ("b", 0), ("rs", 1, 3), ("p", 3, 1), ("rs", 3, 0), ("rs", 1, 4), ("rs", 3, 1),
-    ("rs", 2, 2), ("rs", 1, 5), ("p", 3, 0), ("p", 2, 0), ("rs", 2, 3), ("rs", 3, 2), ("rs", 1, 6), ("rs", 2, 4),
-    ("e", 5), ("rs", 3, 3), ("e", 6), ("e", 7), ("b", 4), ("rs", 3, 4), ("rs", 2, 5), ("rs", 2, 6), ("m", 0, 1), ("b",
-    7), ("rs", 3, 5), ("m", 0, 0), ("b", 5), ("rs", 3, 6), ("fin", 1), ("m", 4, 1), ("c1",), ("m", 4, 0), ("b", 6),
-    ("p", 0, 1), ("rs", 0, 0), ("rs", 0, 1), ("fin", 3), ("m", 7, 1), ("p", 4, 1), ("rs", 4, 0), ("rs", 0, 2), ("rs",
-    4, 1), ("p", 0, 0), ("rs", 0, 3), ("c2",), ("m", 5, 1), ("rs", 0, 4), ("m", 7, 0), ("p", 4, 0), ("rs", 4, 2),
-    ("p", 7, 1), ("rs", 7, 0), ("rs", 7, 1), ("rs", 4, 3), ("m", 6, 1), ("rs", 0, 5), ("m", 5, 0), ("p", 5, 1), ("rs",
-    5, 0), ("rs", 5, 1), ("rs", 7, 2), ("m", 6, 0), ("rs", 4, 4), ("rs", 0, 6), ("rs", 4, 5), ("p", 7, 0), ("rs", 5,
-    2), ("p", 6, 1), ("rs", 6, 0), ("rs", 7, 3), ("rs", 6, 1), ("rs", 7, 4), ("p", 5, 0), ("rs", 5, 3), ("rs", 6, 2),
-    ("rs", 5, 4), ("fin", 0), ("p", 6, 0), ("rs", 6, 3), ("c3",), ("rs", 4, 6), ("rs", 7, 5), ("rs", 6, 4), ("fin",
-    2), ("rs", 7, 6), ("rs", 5, 5), ("rs", 5, 6), ("rs", 6, 5), ("rs", 6, 6), ("fin", 4), ("fin", 7), ("fin", 5),
-    ("fin", 6),
+    ("ag", 0, 0), ("ag", 2, 0), ("meta1",), ("ag", 1, 1), ("ag", 0, 1), ("ag", 0, 2), ("ag", 2, 1), ("ag", 1, 0),
+    ("ag", 0, 3), ("ag", 2, 2), ("ag", 0, 4), ("meta2",), ("ag", 3, 0), ("pick",), ("ag", 2, 3), ("ag", 1, 2), ("ag",
+    0, 5), ("z", 0, 0), ("ag", 2, 4), ("ag", 0, 6), ("ag", 1, 3), ("z", 2, 0), ("ag", 3, 2), ("ag", 1, 4), ("ag", 3,
+    1), ("ag", 2, 6), ("ag", 2, 5), ("ag", 4, 0), ("z", 0, 1), ("rank",), ("z", 1, 0), ("ag", 1, 5), ("ag", 3, 4),
+    ("ag", 1, 6), ("ag", 3, 3), ("z", 2, 1), ("ag", 4, 1), ("ag", 4, 2), ("y", 0), ("ag", 3, 6), ("z", 1, 1), ("ag",
+    3, 5), ("z", 3, 0), ("ag", 4, 4), ("ag", 4, 3), ("ag", 5, 1), ("ag", 5, 0), ("y", 2), ("z", 3, 1), ("ag", 4, 6),
+    ("z", 4, 0), ("ag", 4, 5), ("ag", 6, 1), ("ag", 5, 3), ("ag", 6, 0), ("y", 1), ("z", 4, 1), ("ag", 5, 2), ("y",
+    3), ("ag", 6, 3), ("ag", 6, 2), ("e", 0), ("ag", 5, 4), ("z", 5, 0), ("ag", 5, 5), ("e", 1), ("y", 4), ("ag", 6,
+    4), ("z", 6, 0), ("ag", 5, 6), ("e", 2), ("ag", 6, 5), ("e", 3), ("b", 0), ("ag", 6, 6), ("z", 5, 1), ("b", 2),
+    ("z", 6, 1), ("m", 0, 1), ("y", 5), ("m", 0, 0), ("e", 4), ("y", 6), ("p", 0, 1), ("rs", 0, 0), ("rs", 0, 1),
+    ("m", 2, 1), ("rs", 0, 2), ("m", 2, 0), ("p", 0, 0), ("rs", 0, 3), ("rs", 0, 4), ("b", 1), ("p", 2, 1), ("rs", 2,
+    0), ("rs", 2, 1), ("rs", 0, 6), ("rs", 0, 5), ("e", 5), ("e", 6), ("b", 6), ("p", 2, 0), ("rs", 2, 2), ("rs", 2,
+    3), ("m", 1, 1), ("m", 1, 0), ("b", 3), ("rs", 2, 4), ("c1",), ("rs", 2, 5), ("m", 6, 1), ("b", 5), ("m", 6, 0),
+    ("p", 1, 1), ("rs", 1, 0), ("rs", 1, 1), ("b", 4), ("rs", 2, 6), ("m", 3, 1), ("rs", 1, 2), ("p", 1, 0), ("c2",),
+    ("p", 6, 1), ("rs", 6, 0), ("m", 3, 0), ("rs", 6, 1), ("rs", 1, 3), ("fin", 2), ("fin", 0), ("m", 5, 1), ("rs", 1,
+    4), ("rs", 6, 2), ("p", 3, 1), ("rs", 3, 1), ("rs", 3, 0), ("p", 6, 0), ("rs", 6, 3), ("m", 4, 1), ("rs", 1, 5),
+    ("m", 5, 0), ("rs", 1, 6), ("c3",), ("rs", 6, 4), ("m", 4, 0), ("p", 3, 0), ("rs", 3, 3), ("p", 5, 1), ("rs", 5,
+    0), ("rs", 5, 1), ("rs", 3, 2), ("p", 4, 1), ("rs", 4, 0), ("rs", 4, 1), ("rs", 6, 6), ("rs", 6, 5), ("fin", 1),
+    ("rs", 5, 2), ("rs", 4, 2), ("p", 5, 0), ("rs", 5, 3), ("p", 4, 0), ("rs", 3, 4), ("rs", 4, 3), ("rs", 5, 4),
+    ("rs", 4, 4), ("rs", 3, 5), ("rs", 3, 6), ("rs", 5, 5), ("rs", 5, 6), ("rs", 4, 5), ("rs", 4, 6), ("fin", 3),
+    ("fin", 6), ("fin", 5), ("fin", 4),
 )
 
 

time: 139 us -> 138 us (level)
  no operation moved by 1% of the time
where the time goes in v4:
time: 138 us; the launch traced here: 137 us
  Pallas kernels  134 us (97%)
  local copies, waits for them, and re-layouts  3 us (2%)
    pallas_call x1, Pallas kernels, per_device(): pl.pallas_call(functools.partial(kernel, c, order), out_shape=(jax.ShapeD...  134 us
    unnamed x7, local copies, waits for them, and re-layouts  3 us

profile of v4, /device:TPU:6, one launch (start us, length us, event | category | flops | bytes accessed | tf_op | source)
XLA Modules:
  0.0 137.2 jit_solution(1177899188133207856)
XLA Ops:
  0.6 133.6 %expert_layer.1 = (bf16[128,1024]{1,0:T(8,128)(2,1)}, bf16[128,1024]{1,0:T(8,128)(2,1)}, bf16[8,128]{1,0:T(8,128)(2,1)}) custom-call(bf16[128,1024]{1,0:T(8,128)(2,1)} %x_ref.1, bf16[128,1024]{1,0:T(8,128)(2,1)} %dy_ref.1, bf16[8,128]{1,0:T(8,128)(2,1)} %bitcast.7, s32[4,128]{1,0:T(4,128)} %bitcast.8, s32[8,128]{1,0:T(8,128)} %bitcast.6, s32[1,8]{1,0:T(1,128)} %bitcast.9, ...), custom_call_target="tpu_custom_call" | custom-call | flops 2415919104 | bytes 4194304 | tf_op jit(solution)/shard_map/expert_layer/pallas_call | solution.py:593
  134.2 0.0 copy-start
  134.2 1.7 %copy.15 = bf16[128,1024]{1,0:T(8,128)(2,1)} copy(bf16[128,1024]{1,0:T(8,128)(2,1)} %get-tuple-element.12) | data formatting | bytes 524288
  135.9 0.0 copy-done
  135.9 0.0 copy-start.1
  135.9 0.7 copy.16
  136.6 0.0 copy-done.1
  136.6 0.6 copy.17
Async XLA Ops:
  134.2 1.7 %copy-start = (bf16[128,1024]{1,0:T(8,128)(2,1)S(1)}, bf16[128,1024]{1,0:T(8,128)(2,1)}, u32[]{:S(2)}) copy-start(bf16[128,1024]{1,0:T(8,128)(2,1)} %get-tuple-element.13) | copy-start | bytes 786436
  135.9 0.7 copy-start.1

commit v5 on v4

--- a/solution.py
+++ b/solution.py
@@ -167,6 +167,10 @@
     if d & (d - 1) == 0:
         return v & (d - 1)
     return v - idiv(v, d) * d
+
+
+def far_first(n):
+    return sorted(range(1, n), key=lambda i: (-min(i, n - i), i))
 
 
 def onehot(mask):
@@ -391,7 +395,7 @@
         width = c.inp[s][2]
         rows = xg[s][ch * PC:(ch + 1) * PC].reshape(PC * TOK, width)
         zs[s][ch] = mm(pick[ch], rows).astype(BF).reshape(NQ, BL, width)
-        for i in range(1, NQ):
+        for i in far_first(NQ):
             q, to = q_peer(i)
             copy(zs[s].at[ch, q], zr[s].at[ch, b_me], z_s.at[s, ch], z_r.at[s, ch], to, y).start()
         zr[s][ch, b_me] = zs[s][ch, b_me]
@@ -401,7 +405,7 @@
         for ch in range(2):
             await_recv(zr[s].at[ch, pl.ds(0, NQ - 1)], z_r.at[s, ch])
         ys[s][...] = mm(sel[...].reshape(R, I), zr[s][...].reshape(I, width)).astype(BF).reshape(NL, Q, width)
-        for i in range(1, NL):
+        for i in far_first(NL):
             to = y_peer(i)
             copy(ys[s].at[to], yr[s].at[y], y_s.at[s], y_r.at[s], node, to).start()
         yr[s][y] = ys[s][y]
@@ -440,7 +444,7 @@
         else:
             value = mm_nt(g_g[...], wg[cols]) + mm_nt(g_u[...], wu[cols])
         bs[u][...] = value.astype(BF).reshape(NL, Q, width)
-        for i in range(1, NL):
+        for i in far_first(NL):
             to = y_peer(i)
             copy(bs[u].at[to], br[u].at[y], b_s.at[u], b_r.at[u], node, to).start()
         br[u][y] = bs[u][y]
@@ -454,7 +458,7 @@
             await_recv(br[u].at[pl.ds(0, NL - 1)], b_r.at[u])
         half = I // 2
         rzs[u][ch] = mm(selg[ch * half:(ch + 1) * half], br[u][...].reshape(R, width)).astype(BF).reshape(NQ, BL, width)
-        for i in range(1, NQ):
+        for i in far_first(NQ):
             q, to = q_peer(i)
             copy(rzs[u].at[ch, q], rzr[u].at[ch, b_me], rz_s.at[u, ch], rz_r.at[u, ch], to, y).start()
         rzr[u][ch, b_me] = rzs[u][ch, b_me]
@@ -505,7 +509,7 @@
         fold = onehot(iota((n, I), 0) == slot_rows(iota((n, I), 1)))
         cm[...] = mm(fold, got).reshape(NQ, NX, LANES)
         c1r[b_me] = cm[b_me]
-        for i in range(1, NQ):
+        for i in far_first(NQ):
             q, to = q_peer(i)
             copy(cm.at[q], c1r.at[b_me], s_small.at[2], r_small.at[2], to, y).start()
 

time: 138 us -> 134 us (0.971)
  Pallas kernels: 134 us -> 130 us
    pallas_call x1, Pallas kernels: 134 us -> 130 us  [per_device(): pl.pallas_call(functools.partial(kernel, c, order), out_shape=(jax.ShapeD...]
where the time goes in v5:
time: 134 us
  Pallas kernels  130 us (97%)
  local copies, waits for them, and re-layouts  3 us (2%)
    pallas_call x1, Pallas kernels, per_device(): pl.pallas_call(functools.partial(kernel, c, order), out_shape=(jax.ShapeD...  130 us
    unnamed x7, local copies, waits for them, and re-layouts  3 us

profile of v5, /device:TPU:6, one launch (start us, length us, event | category | flops | bytes accessed | tf_op | source)
XLA Modules:
  0.0 133.7 jit_solution(3660833068336597694)
XLA Ops:
  0.6 130.0 %expert_layer.1 = (bf16[128,1024]{1,0:T(8,128)(2,1)}, bf16[128,1024]{1,0:T(8,128)(2,1)}, bf16[8,128]{1,0:T(8,128)(2,1)}) custom-call(bf16[128,1024]{1,0:T(8,128)(2,1)} %x_ref.1, bf16[128,1024]{1,0:T(8,128)(2,1)} %dy_ref.1, bf16[8,128]{1,0:T(8,128)(2,1)} %bitcast.7, s32[4,128]{1,0:T(4,128)} %bitcast.8, s32[8,128]{1,0:T(8,128)} %bitcast.6, s32[1,8]{1,0:T(1,128)} %bitcast.9, ...), custom_call_target="tpu_custom_call" | custom-call | flops 2415919104 | bytes 4194304 | tf_op jit(solution)/shard_map/expert_layer/pallas_call | solution.py:597
  130.6 0.0 copy-start
  130.7 1.7 %copy.15 = bf16[128,1024]{1,0:T(8,128)(2,1)} copy(bf16[128,1024]{1,0:T(8,128)(2,1)} %get-tuple-element.12) | data formatting | bytes 524288
  132.4 0.0 copy-done
  132.4 0.0 copy-start.1
  132.4 0.7 copy.16
  133.1 0.0 copy-done.1
  133.1 0.6 copy.17
Async XLA Ops:
  130.6 1.7 %copy-start = (bf16[128,1024]{1,0:T(8,128)(2,1)S(1)}, bf16[128,1024]{1,0:T(8,128)(2,1)}, u32[]{:S(2)}) copy-start(bf16[128,1024]{1,0:T(8,128)(2,1)} %get-tuple-element.13) | copy-start | bytes 786436
  132.4 0.7 copy-start.1
